TPU v7x, 128 devices: a whole 4x4x4 slice. The times are simulated.
128 devices in a mesh: row: 8 (over y, z_hi), col: 16 (over z_lo, x, core).
Axes of the slice: x: 4, y: 4, z: 4 (z_hi: 2, z_lo: 2; z = z_hi * 2 + z_lo), core: 2. Of those that a mesh axis runs over, the one named last changes fastest.
Arguments:
- inputs: bfloat16 [768, 12288], P('row', 'col'), may hold values from -6 to 6
- out_grad: bfloat16 [768, 12288], P('row', 'col'), may hold values from -6 to 6
- gate_pre: bfloat16 [768, 24576], P('col', 'row'), may hold values from -8 to 8
- up_pre: bfloat16 [768, 24576], P('col', 'row'), may hold values from -6 to 6
- gate_weight: bfloat16 [12288, 24576], P('col', 'row'), may hold values from -0.0546875 to 0.0546875
- up_weight: bfloat16 [12288, 24576], P('col', 'row'), may hold values from -0.0546875 to 0.0546875
- down_weight: bfloat16 [24576, 12288], P('row', 'col'), may hold values from -0.0390625 to 0.0390625
Outputs:
- grad_input: bfloat16 [768, 12288], P('row', 'col')
- grad_gate: bfloat16 [12288, 24576], P('col', 'row')
- grad_up: bfloat16 [12288, 24576], P('col', 'row')
All inputs are finite; a program needn't handle non-finite values.
Results may differ from a plain program's by a relative error of at most 0.0049.
Values may be sent and summed in bfloat16 or wider, within the bound.
A program may use at most 128 MiB of HBM per device.

v0:
```python
import jax
import jax.numpy as jnp
from jax import lax
from jax.sharding import PartitionSpec as P


def swiglu_back(hidden_delta, gate_pre, up_pre):
    gate_vals = gate_pre.astype(jnp.float32)
    up_vals = up_pre.astype(jnp.float32)
    sigma = jax.nn.sigmoid(gate_vals)
    up_delta = (hidden_delta * gate_vals * sigma).astype(jnp.bfloat16)
    gate_delta = (hidden_delta * up_vals * sigma * (1.0 + gate_vals * (1.0 - sigma))).astype(
        jnp.bfloat16
    )
    return (gate_delta, up_delta)


def right_trans(left, right):
    return lax.dot_general(
        left, right, (((1,), (1,)), ((), ())), preferred_element_type=jnp.float32
    )


def left_trans(left, right):
    return lax.dot_general(
        left, right, (((0,), (0,)), ((), ())), preferred_element_type=jnp.float32
    )


def on_device(inputs, out_grad, gate_pre, up_pre, gate_weight, up_weight, down_weight):
    input_cols, grad_cols = (
        lax.all_gather(inputs, "row", axis=0, tiled=True),
        lax.all_gather(out_grad, "row", axis=0, tiled=True),
    )
    hidden_delta = lax.psum_scatter(
        right_trans(grad_cols, down_weight), "col", scatter_dimension=0, tiled=True
    )
    gate_local, up_local = swiglu_back(hidden_delta, gate_pre, up_pre)
    gate_delta, up_delta = (
        lax.all_gather(gate_local, "col", axis=0, tiled=True),
        lax.all_gather(up_local, "col", axis=0, tiled=True),
    )
    grad_input = lax.psum_scatter(
        right_trans(gate_delta, gate_weight) + right_trans(up_delta, up_weight),
        "row",
        scatter_dimension=0,
        tiled=True,
    ).astype(jnp.bfloat16)
    grad_gate = left_trans(input_cols, gate_delta).astype(jnp.bfloat16)
    grad_up = left_trans(input_cols, up_delta).astype(jnp.bfloat16)
    return (grad_input, grad_gate, grad_up)


def solution(mesh):
    placed = (
        P("row", "col"),
        P("row", "col"),
        P("col", "row"),
        P("col", "row"),
        P("col", "row"),
        P("col", "row"),
        P("row", "col"),
    )
    return jax.shard_map(
        on_device,
        mesh=mesh,
        in_specs=placed,
        out_specs=(P("row", "col"), P("col", "row"), P("col", "row")),
        check_vma=False,
    )
```

profile of v0, /device:TPU:1, one launch (start us, length us, event | category | flops | bytes accessed | tf_op | source)
XLA Modules:
  0.0 365.2 jit_solution(3973554252166828644)
XLA Ops:
  7.2 0.0 all-gather.5.cloned.1.call-start
  7.2 0.7 all-gather.5.cloned.1.call-update
  7.9 0.0 reduce-scatter.3.cloned.1.call-start
  7.9 52.5 %all-gather.5.cloned.1.call-done = bf16[768,768]{1,0:T(8,128)(2,1)} async-done(((bf16[96,768]{1,0:T(8,128)(2,1)}), bf16[768,768]{1,0:T(8,128)(2,1)}) %all-gather.5.cloned.1.call-update) | async-done | bytes 1179664 | tf_op jit(solution)/shard_map/all_gather | solution.py:33
  60.4 10.2 %fusion.10 = f32[768,3072]{1,0:T(8,128)} fusion(bf16[768,768]{1,0:T(8,128)(2,1)} %all-gather.5.cloned.1.call-done, bf16[3072,768]{1,0:T(8,128)(2,1)} %param.13), kind=kOutput, calls=%fused_computation.16 | convolution fusion | flops 3623878656 | bytes 15335424 | tf_op jit(solution)/shard_map/dot_general | solution.py:19
  70.6 0.0 copy-start
  70.6 0.0 copy-start.1
  70.6 0.0 reduce-scatter.3.cloned.1.call-update
  70.7 0.0 all-gather.7.cloned.1.call-start
  70.7 73.9 %reduce-scatter.3.cloned.1.call-done = f32[48,3072]{1,0:T(8,128)} async-done(((f32[768,3072]{1,0:T(8,128)}), f32[48,3072]{1,0:T(8,128)}) %reduce-scatter.3.cloned.1.call-update) | async-done | bytes 589840 | tf_op jit(solution)/shard_map/reduce_scatter | solution.py:35
  144.6 0.0 copy-done
  144.6 0.0 copy-done.1
  144.6 2.2 fusion.9
  146.8 0.0 all-gather.7.cloned.1.call-update
  146.8 0.0 all-gather.9.cloned.1.call-start
  146.9 0.5 all-gather.9.cloned.1.call-update
  147.4 0.0 all-gather.11.cloned.1.call-start
  147.4 0.5 all-gather.11.cloned.1.call-update
  148.0 0.2 reduce-scatter.5.cloned.1.call-start
  148.2 39.2 %all-gather.7.cloned.1.call-done = bf16[768,3072]{1,0:T(8,128)(2,1)} async-done(((bf16[48,3072]{1,0:T(8,128)(2,1)}), bf16[768,3072]{1,0:T(8,128)(2,1)}) %all-gather.7.cloned.1.call-update) | async-done | bytes 4718608 | tf_op jit(solution)/shard_map/all_gather | solution.py:40
  187.4 7.1 %fusion.11 = f32[768,768]{1,0:T(8,128)S(1)} fusion(bf16[768,3072]{1,0:T(8,128)(2,1)} %all-gather.7.cloned.1.call-done, bf16[768,3072]{1,0:T(8,128)(2,1)} %param.11), kind=kOutput, calls=%fused_computation.17 | convolution fusion | flops 3623878656 | bytes 11796480 | tf_op jit(solution)/shard_map/dot_general | solution.py:19
  194.6 33.5 %all-gather.9.cloned.1.call-done = bf16[768,3072]{1,0:T(8,128)(2,1)} async-done(((bf16[48,3072]{1,0:T(8,128)(2,1)}), bf16[768,3072]{1,0:T(8,128)(2,1)}) %all-gather.9.cloned.1.call-update) | async-done | bytes 4718608 | tf_op jit(solution)/shard_map/all_gather | solution.py:41
  228.1 9.0 %convolution_add_fusion = f32[768,768]{1,0:T(8,128)} fusion(f32[768,768]{1,0:T(8,128)S(1)} %fusion.11, bf16[768,3072]{1,0:T(8,128)(2,1)} %all-gather.9.cloned.1.call-done, bf16[768,3072]{1,0:T(8,128)(2,1)} %param.12), kind=kOutput, calls=%fused_computation.4 | convolution fusion | flops 3624468480 | bytes 14155776 | tf_op jit(solution)/shard_map/dot_general | solution.py:19
  237.1 0.0 reduce-scatter.5.cloned.1.call-update
  237.2 39.7 %all-gather.11.cloned.1.call-done = bf16[768,768]{1,0:T(8,128)(2,1)} async-done(((bf16[96,768]{1,0:T(8,128)(2,1)}), bf16[768,768]{1,0:T(8,128)(2,1)}) %all-gather.11.cloned.1.call-update) | async-done | bytes 1179664 | tf_op jit(solution)/shard_map/all_gather | solution.py:32
  276.9 8.8 %fusion = bf16[768,3072]{0,1:T(8,128)(2,1)} fusion(bf16[768,3072]{1,0:T(8,128)(2,1)} %all-gather.7.cloned.1.call-done, bf16[768,768]{1,0:T(8,128)(2,1)} %all-gather.11.cloned.1.call-done), kind=kOutput, calls=%fused_computation.2 | convolution fusion | flops 3626237952 | bytes 10616832 | tf_op jit(solution)/shard_map/dot_general | solution.py:25
  285.7 0.0 copy-start.2
  285.7 6.7 %copy.10 = bf16[768,3072]{1,0:T(8,128)(2,1)} copy(bf16[768,3072]{0,1:T(8,128)(2,1)} %fusion) | data formatting | bytes 9437184
  292.4 0.0 copy-done.2
  292.4 8.0 %fusion.1 = bf16[768,3072]{0,1:T(8,128)(2,1)} fusion(bf16[768,3072]{1,0:T(8,128)(2,1)} %all-gather.9.cloned.1.call-done, bf16[768,768]{1,0:T(8,128)(2,1)S(1)} %copy-done.2), kind=kOutput, calls=%fused_computation.3 | convolution fusion | flops 3626237952 | bytes 10616832 | tf_op jit(solution)/shard_map/dot_general | solution.py:25
  300.4 6.6 %copy.11 = bf16[768,3072]{1,0:T(8,128)(2,1)} copy(bf16[768,3072]{0,1:T(8,128)(2,1)} %fusion.1) | data formatting | bytes 9437184
  307.1 49.7 %reduce-scatter.5.cloned.1.call-done = f32[96,768]{1,0:T(8,128)} async-done(((f32[768,768]{1,0:T(8,128)}), f32[96,768]{1,0:T(8,128)}) %reduce-scatter.5.cloned.1.call-update) | async-done | bytes 294928 | tf_op jit(solution)/shard_map/reduce_scatter | solution.py:43
  356.7 1.6 convert_element_type.31
Async XLA Ops:
  7.2 53.3 %all-gather.5.cloned.1.call-start = ((), (), s32[]{:S(2)}) async-start(), calls=%async_computation.2 | async-start | bytes 1327104 | tf_op jit(solution)/shard_map/all_gather | solution.py:33
  7.9 136.7 %reduce-scatter.3.cloned.1.call-start = ((), (), s32[]{:S(2)}) async-start(), calls=%async_computation.3 | async-start | bytes 10027008 | tf_op jit(solution)/shard_map/reduce_scatter | solution.py:35
  70.6 74.0 %copy-start = (bf16[48,3072]{1,0:T(8,128)(2,1)S(1)}, bf16[48,3072]{1,0:T(8,128)(2,1)}, u32[]{:S(2)}) copy-start(bf16[48,3072]{1,0:T(8,128)(2,1)} %param.9) | copy-start | bytes 884740
  70.6 74.0 %copy-start.1 = (bf16[48,3072]{1,0:T(8,128)(2,1)S(1)}, bf16[48,3072]{1,0:T(8,128)(2,1)}, u32[]{:S(2)}) copy-start(bf16[48,3072]{1,0:T(8,128)(2,1)} %param.10) | copy-start | bytes 884740
  70.7 116.8 %all-gather.7.cloned.1.call-start = ((), (), s32[]{:S(2)}) async-start(), calls=%async_computation.4 | async-start | bytes 5013504 | tf_op jit(solution)/shard_map/all_gather | solution.py:40
  146.8 81.3 %all-gather.9.cloned.1.call-start = ((), (), s32[]{:S(2)}) async-start(), calls=%async_computation.5 | async-start | bytes 5013504 | tf_op jit(solution)/shard_map/all_gather | solution.py:41
  147.4 129.5 %all-gather.11.cloned.1.call-start = ((), (), s32[]{:S(2)}) async-start(), calls=%async_computation.7 | async-start | bytes 1327104 | tf_op jit(solution)/shard_map/all_gather | solution.py:32
  148.0 208.8 %reduce-scatter.5.cloned.1.call-start = ((), (), s32[]{:S(2)}) async-start(), calls=%async_computation.6 | async-start | bytes 2654208 | tf_op jit(solution)/shard_map/reduce_scatter | solution.py:43
  285.7 6.7 %copy-start.2 = (bf16[768,768]{1,0:T(8,128)(2,1)S(1)}, bf16[768,768]{1,0:T(8,128)(2,1)}, u32[]{:S(2)}) copy-start(bf16[768,768]{1,0:T(8,128)(2,1)} %all-gather.11.cloned.1.call-done) | copy-start | bytes 3538948
Sparse Core Ops, SparseCore 0:
  10.3 50.0 all-gather.4
  70.8 73.7 reduce-scatter.2
  146.9 40.4 all-gather.6
  189.6 38.4 all-gather.8
  230.3 46.5 all-gather.10
  280.6 76.1 reduce-scatter.4
where the time goes:
time: 366 us; the launch traced here: 365 us
  waiting for transfers between devices  290 us (79%)
  matrix products  43.2 us (12%)
  between operations  14.1 us (4%)
  local copies, waits for them, and re-layouts  13.4 us (4%)
  other arithmetic  3.8 us (1%)
    reduce_scatter x1, waiting for transfers between devices, on_device(): lax.psum_scatter(right_trans(grad_cols, down_weight), 'col', scatter_dime...  73.9 us
    all_gather x1, waiting for transfers between devices, on_device(): lax.all_gather(out_grad, 'row', axis=0, tiled=True)  52.5 us
    reduce_scatter x1, waiting for transfers between devices, on_device(): lax.psum_scatter(right_trans(gate_delta, gate_weight) + right_trans(up_de...  49.7 us
    all_gather x1, waiting for transfers between devices, on_device(): lax.all_gather(inputs, 'row', axis=0, tiled=True)  39.7 us
    all_gather x1, waiting for transfers between devices, on_device(): lax.all_gather(gate_local, 'col', axis=0, tiled=True)  39.2 us
    all_gather x1, waiting for transfers between devices, on_device(): lax.all_gather(up_local, 'col', axis=0, tiled=True)  33.5 us
    dot_general x3, matrix products, right_trans(): lax.dot_general(left, right, (((1,), (1,)), ((), ())), preferred_element_...  26.4 us
    dot_general x2, matrix products, left_trans(): lax.dot_general(left, right, (((0,), (0,)), ((), ())), preferred_element_...  16.8 us
  transfers between devices with their start and end apart: 6, of which 6 were waited for; matrix products, arithmetic and copies ran while one was open for 13% of the time, Pallas kernels for 0%

commit v1 on v0

v1 whole, which is shorter than its diff:
```python
import jax
import jax.numpy as jnp
from jax import lax
from jax.experimental import pallas as pl
from jax.experimental.pallas import tpu as pltpu
from jax.sharding import PartitionSpec as P

BF16 = jnp.bfloat16
F32 = jnp.float32
NY, NZH, NZL, NX, NK = 4, 2, 2, 4, 2
NP = NZL * NX
NJ = 3
NH = 2
TB = 16


def right_trans(left, right):
    return lax.dot_general(
        left, right, (((1,), (1,)), ((), ())), preferred_element_type=F32
    )


def left_trans(left, right):
    return lax.dot_general(
        left, right, (((0,), (0,)), ((), ())), preferred_element_type=F32
    )


def kernel(
    og_ref,
    in_ref,
    gp_ref,
    up_ref,
    gw_ref,
    uw_ref,
    dw_ref,
    gi_ref,
    dg_ref,
    du_ref,
    xg_ref,
    dwv,
    gwv,
    uwv,
    gpv,
    upv,
    og,
    xg,
    db,
    hs,
    hr,
    ho,
    zs,
    zr,
    xs,
    xr,
    gacc,
    gs,
    gr,
    gz,
    gzr,
    load_sem,
    s_og,
    r_og,
    s_in,
    r_in,
    s_rs,
    r_rs,
    s_ag,
    r_ag,
    s_gi,
    r_gi,
    out_sem,
):
    r = lax.axis_index("row")
    c = lax.axis_index("col")
    y, zh = r // 2, r % 2
    zl, x, k = c // 8, (c // 2) % 4, c % 2
    p = zl * NX + x
    pz = (1 - zl) * NX + x

    def xmod(d):
        return (x + d) % NX

    dev_k = (r, c + 1 - 2 * k)
    dev_zl = (r, (1 - zl) * 8 + x * 2 + k)
    dev_zh = (y * 2 + 1 - zh, c)

    def dev_x(d):
        return (r, zl * 8 + xmod(d) * 2 + k)

    def dev_y(d):
        return (((y + d) % NY) * 2 + zh, c)

    ff = dw_ref.shape[0]
    dl = dw_ref.shape[1]
    cw = ff // NH

    barrier = pltpu.get_barrier_semaphore()
    peers = [dev_k, dev_zl, dev_zh] + [dev_x(d) for d in (1, 2, 3)] + [dev_y(d) for d in (1, 2, 3)]
    for dev in peers:
        pl.semaphore_signal(barrier, 1, device_id=dev, device_id_type=pl.DeviceIdType.MESH)

    loads = {}

    def load(name, src, dst):
        cp = pltpu.make_async_copy(src, dst, load_sem.at[len(loads)])
        cp.start()
        loads[name] = cp

    load("og", og_ref, og.at[r])
    load("dw", dw_ref, dwv)
    load("in", in_ref, xg.at[r])
    load("gp", gp_ref, gpv)
    load("up", up_ref, upv)
    load("gw", gw_ref, gwv)
    load("uw", uw_ref, uwv)

    pl.semaphore_wait(barrier, len(peers))

    sent = []

    def send(src, dst, ssem, rsem, dev):
        cp = pltpu.make_async_remote_copy(
            src_ref=src,
            dst_ref=dst,
            send_sem=ssem,
            recv_sem=rsem,
            device_id=dev,
            device_id_type=pl.DeviceIdType.MESH,
        )
        cp.start()
        sent.append(cp)
        return cp

    ogc = {}
    for j in range(NJ):
        for n, dev in enumerate([dev_zh] + [dev_y(d) for d in (1, 2, 3)]):
            ogc[j, n] = send(og_ref.at[:, j], og.at[r, :, j], s_og.at[j, n], r_og.at[j, n], dev)
    rz = y * 2 + 1 - zh
    for j in range(NJ):
        ogc[j, 0].wait_recv()
        for n, d in enumerate((1, 2, 3)):
            ogc[j, 4 + n] = send(
                og.at[rz, :, j], og.at[rz, :, j], s_og.at[j, 4 + n], r_og.at[j, 4 + n], dev_y(d)
            )
    inc = {}
    inc[0] = send(in_ref, xg.at[r], s_in.at[0], r_in.at[0], dev_zh)

    rs = {}
    ag = {}
    gic = {}

    def cols(h):
        return pl.ds(h * cw, cw)

    def s0(j, h):
        if h == 0:
            for n in range(1, 7):
                ogc[j, n].wait_recv()
        u = j * NH + h
        left = jnp.concatenate(
            [og[:, 1 - k, j].reshape(NP * TB, dl), og[:, k, j].reshape(NP * TB, dl)], axis=0
        )
        nt = 512

        def tile(n, _):
            w = dwv[pl.ds(pl.multiple_of(h * cw + n * nt, nt), nt), :]
            out = right_trans(left, w)
            at = pl.ds(pl.multiple_of(n * nt, nt), nt)
            hs[u, :, :, at] = out[: NP * TB].astype(BF16).reshape(NP, TB, nt)
            ho[u, :, :, at] = out[NP * TB :].reshape(NP, TB, nt)
            return 0

        lax.fori_loop(0, cw // nt, tile, 0)
        rs[u, 0] = send(hs.at[u], hr.at[u], s_rs.at[u, 0], r_rs.at[u, 0], dev_k)

    def s1(j, h):
        u = j * NH + h
        rs[u, 0].wait_recv()

        def add(i, _):
            far = (1 - zl) * NX + i
            zs[u, i] = (ho[u, far] + hr[u, far].astype(F32)).astype(BF16)
            return 0

        lax.fori_loop(0, NX, add, 0)
        rs[u, 1] = send(zs.at[u], zr.at[u], s_rs.at[u, 1], r_rs.at[u, 1], dev_zl)

    def s2(j, h):
        u = j * NH + h
        rs[u, 1].wait_recv()
        for d in (1, 3, 2):
            q = xmod(d)
            near = zl * NX + q
            xs[u, d - 1] = (
                ho[u, near] + hr[u, near].astype(F32) + zr[u, q].astype(F32)
            ).astype(BF16)
            rs[u, 1 + d] = send(
                xs.at[u, d - 1], xr.at[u, d - 1], s_rs.at[u, 1 + d], r_rs.at[u, 1 + d], dev_x(d)
            )

    def piece(q, j, h):
        return db.at[:, q, k, j, :, cols(h)]

    def part(a, q, j, h):
        return db.at[a, q, k, j, :, cols(h)]

    def ag_send(u, n, ref, dev):
        ag[u, n] = send(ref, ref, s_ag.at[u, n], r_ag.at[u, n], dev)

    def s3(j, h):
        u = j * NH + h
        for d in (1, 3, 2):
            rs[u, 1 + d].wait_recv()
        hidden = ho[u, p] + hr[u, p].astype(F32) + zr[u, x].astype(F32)
        for d in (1, 2, 3):
            hidden = hidden + xr[u, d - 1].astype(F32)
        g = gpv[j, :, cols(h)].astype(F32)
        up = upv[j, :, cols(h)].astype(F32)
        s = jax.nn.sigmoid(g)
        db[1, p, k, j, :, cols(h)] = (hidden * g * s).astype(BF16)
        db[0, p, k, j, :, cols(h)] = (hidden * up * s * (1.0 + g * (1.0 - s))).astype(BF16)
        ref = piece(p, j, h)
        ag_send(u, 0, ref, dev_zl)
        ag_send(u, 1, ref, dev_x(1))
        ag_send(u, 2, ref, dev_x(3))
        ag_send(u, 3, ref, dev_k)

    def s4(j, h):
        u = j * NH + h
        ag[u, 0].wait_recv()
        ref = piece(pz, j, h)
        ag_send(u, 4, ref, dev_x(1))
        ag_send(u, 5, ref, dev_x(3))
        ag_send(u, 6, ref, dev_k)

    def relay(j, h, first, base, lane):
        u = j * NH + h
        lo = lane * NX + xmod(3)
        hi = lane * NX + xmod(1)
        ag[u, first].wait_recv()
        ag_send(u, base, part(0, lo, j, h), dev_x(1))
        ag_send(u, base + 1, piece(lo, j, h), dev_k)
        ag[u, first + 1].wait_recv()
        ag_send(u, base + 2, part(1, hi, j, h), dev_x(3))
        ag_send(u, base + 3, piece(hi, j, h), dev_k)

    def s5(j, h):
        relay(j, h, 1, 7, zl)

    def s6(j, h):
        relay(j, h, 4, 11, 1 - zl)

    def s7(j, h):
        u = j * NH + h
        ag[u, 7].wait_recv()
        ag[u, 9].wait_recv()
        ag_send(u, 15, piece(zl * NX + xmod(2), j, h), dev_k)

    def s8(j, h):
        u = j * NH + h
        ag[u, 11].wait_recv()
        ag[u, 13].wait_recv()
        ag_send(u, 16, piece((1 - zl) * NX + xmod(2), j, h), dev_k)

    outs = []

    def s9(j, h):
        u = j * NH + h
        for n in (3, 6, 8, 10, 12, 14, 15, 16):
            ag[u, n].wait_recv()
        for a, ref in ((0, dg_ref), (1, du_ref)):
            cp = pltpu.make_async_copy(
                db.at[a, :, :, j, :, cols(h)], ref.at[:, :, j, :, cols(h)], out_sem.at[u, a]
            )
            cp.start()
            outs.append(cp)
        nt = 256
        dgate = db[0, :, :, j, :, cols(h)].reshape(NP * NK * TB, cw)
        dup = db[1, :, :, j, :, cols(h)].reshape(NP * NK * TB, cw)

        def tile(n, _):
            rows = pl.ds(pl.multiple_of(n * nt, nt), nt)
            out = right_trans(dgate, gwv[rows, cols(h)]) + right_trans(dup, uwv[rows, cols(h)])
            if h > 0:
                out = out + gacc[j, :, rows]
            if h < NH - 1:
                gacc[j, :, rows] = out
            else:
                gacc[j, :, rows] = out
                gs[j, :, :, :, rows] = out.astype(BF16).reshape(NP, NK, TB, nt)
            return 0

        lax.fori_loop(0, dl // nt, tile, 0)
        if h == NH - 1:
            for d in (1, 3, 2):
                to = (y + d) % NY
                gic[j, d] = send(
                    gs.at[j, pl.ds(to * 2, 2)],
                    gr.at[j, d - 1],
                    s_gi.at[j, d],
                    r_gi.at[j, d],
                    dev_y(d),
                )

    def s10(j, h):
        for d in (1, 3, 2):
            gic[j, d].wait_recv()

        def total(q):
            own = gacc[j, pl.ds(pl.multiple_of((y * 2 + q) * NK * TB, NK * TB), NK * TB), :]
            acc = own.reshape(NK, TB, dl)
            for d in (1, 2, 3):
                acc = acc + gr[j, d - 1, q].astype(F32)
            return acc

        gz[j] = total(1 - zh).astype(BF16)
        gic[j, 0] = send(gz.at[j], gzr.at[j], s_gi.at[j, 0], r_gi.at[j, 0], dev_zh)
        own = total(zh)
        gacc[j, pl.ds(0, NK * TB), :] = own.reshape(NK * TB, dl)

    def s11(j, h):
        gic[j, 0].wait_recv()
        own = gacc[j, pl.ds(0, NK * TB), :].reshape(NK, TB, dl)
        gi_ref[:, j] = (own + gzr[j].astype(F32)).astype(BF16)

    def inputs_on():
        inc[0].wait_recv()
        loads["in"].wait()
        for n, d in enumerate((1, 2, 3)):
            ref = xg.at[pl.ds(y * 2, 2)]
            inc[1 + n] = send(ref, ref, s_in.at[1 + n], r_in.at[1 + n], dev_y(d))

    def inputs_done():
        for n in range(3):
            inc[1 + n].wait_recv()
        cp = pltpu.make_async_copy(xg, xg_ref, out_sem.at[NJ * NH, 0])
        cp.start()
        outs.append(cp)

    steps = [s0, s1, s2, s3, s4, s5, s6, s7, s8, s9]
    units = [(j, h) for j in range(NJ) for h in range(NH)]

    loads["og"].wait()
    loads["dw"].wait()
    lag = [0, 1, 2, 3, 4, 5, 6, 7, 8, 9]
    nu = len(units)
    done = set()
    for t in range(nu + lag[-1]):
        for n in reversed(range(len(steps))):
            i = t - lag[n]
            if 0 <= i < nu:
                if n == 3 and i == 0:
                    loads["gp"].wait()
                    loads["up"].wait()
                if n == 9 and i == 0:
                    loads["gw"].wait()
                    loads["uw"].wait()
                steps[n](*units[i])
        if t == 2:
            inputs_on()
        if t == 10:
            inputs_done()
        for j in range(NJ):
            last = lag[-1] + (j + 1) * NH - 1
            if t == last + 1 and t < nu + lag[-1]:
                s10(j, 0)
                done.add(j)
    for j in range(NJ):
        if j not in done:
            s10(j, 0)
    for j in range(NJ):
        s11(j, 0)
    for cp in outs:
        cp.wait()
    for cp in sent:
        cp.wait_send()


def exchange(out_grad, inputs, gate_pre, up_pre, gate_weight, up_weight, down_weight):
    ff, dl = down_weight.shape
    cw = ff // NH
    nu = NJ * NH
    tok = NP * NK * NJ * TB
    dma = pltpu.SemaphoreType.DMA
    vm = pltpu.VMEM
    hbm = pl.BlockSpec(memory_space=pl.ANY)
    outs = pl.pallas_call(
        kernel,
        out_shape=(
            jax.ShapeDtypeStruct((NK, NJ, TB, dl), BF16),
            jax.ShapeDtypeStruct((NP, NK, NJ, TB, ff), BF16),
            jax.ShapeDtypeStruct((NP, NK, NJ, TB, ff), BF16),
            jax.ShapeDtypeStruct((NP, NK, NJ, TB, dl), BF16),
        ),
        in_specs=[hbm] * 7,
        out_specs=(pl.BlockSpec(memory_space=pltpu.VMEM), hbm, hbm, hbm),
        scratch_shapes=[
            vm((ff, dl), BF16),
            vm((dl, ff), BF16),
            vm((dl, ff), BF16),
            vm((NJ, TB, ff), BF16),
            vm((NJ, TB, ff), BF16),
            vm((NP, NK, NJ, TB, dl), BF16),
            vm((NP, NK, NJ, TB, dl), BF16),
            vm((2, NP, NK, NJ, TB, ff), BF16),
            vm((nu, NP, TB, cw), BF16),
            vm((nu, NP, TB, cw), BF16),
            vm((nu, NP, TB, cw), F32),
            vm((nu, NX, TB, cw), BF16),
            vm((nu, NX, TB, cw), BF16),
            vm((nu, 3, TB, cw), BF16),
            vm((nu, 3, TB, cw), BF16),
            vm((NJ, NP * NK * TB, dl), F32),
            vm((NJ, NP, NK, TB, dl), BF16),
            vm((NJ, 3, 2, NK, TB, dl), BF16),
            vm((NJ, NK, TB, dl), BF16),
            vm((NJ, NK, TB, dl), BF16),
            dma((7,)),
            dma((NJ, 7)),
            dma((NJ, 7)),
            dma((4,)),
            dma((4,)),
            dma((nu, 5)),
            dma((nu, 5)),
            dma((nu, 17)),
            dma((nu, 17)),
            dma((NJ, 4)),
            dma((NJ, 4)),
            dma((nu + 1, 2)),
        ],
        compiler_params=pltpu.CompilerParams(
            collective_id=0, has_side_effects=True, vmem_limit_bytes=62 * 2**20
        ),
        cost_estimate=pl.CostEstimate(
            flops=6 * tok * dl * ff, bytes_accessed=16 * dl * ff, transcendentals=0
        ),
    )(
        out_grad.reshape(NK, NJ, TB, dl),
        inputs.reshape(NK, NJ, TB, dl),
        gate_pre.reshape(NJ, TB, ff),
        up_pre.reshape(NJ, TB, ff),
        gate_weight,
        up_weight,
        down_weight,
    )
    grad_input, gate_delta, up_delta, tokens = outs
    return (
        grad_input.reshape(NK * NJ * TB, dl),
        gate_delta.reshape(tok, ff),
        up_delta.reshape(tok, ff),
        tokens.reshape(tok, dl),
    )


def on_device(inputs, out_grad, gate_pre, up_pre, gate_weight, up_weight, down_weight):
    grad_input, gate_delta, up_delta, tokens = exchange(
        out_grad, inputs, gate_pre, up_pre, gate_weight, up_weight, down_weight
    )
    grad_gate = left_trans(tokens, gate_delta).astype(BF16)
    grad_up = left_trans(tokens, up_delta).astype(BF16)
    return (grad_input, grad_gate, grad_up)


def solution(mesh):
    placed = (
        P("row", "col"),
        P("row", "col"),
        P("col", "row"),
        P("col", "row"),
        P("col", "row"),
        P("col", "row"),
        P("row", "col"),
    )
    return jax.shard_map(
        on_device,
        mesh=mesh,
        in_specs=placed,
        out_specs=(P("row", "col"), P("col", "row"), P("col", "row")),
        check_vma=False,
    )
```

time: 366 us -> 124 us (0.34)
  waiting for transfers between devices: 290 us -> 0 us
  Pallas kernels: 0 us -> 106 us
  matrix products: 43.2 us -> 14.5 us
  between operations: 14.1 us -> 0.66 us
  local copies, waits for them, and re-layouts: 13.4 us -> 0.67 us
  other arithmetic: 3.8 us -> 0 us
    all_gather x4 -> x0, waiting for transfers between devices: 165 us -> none  [the longest x1 52.5 us: on_device(): lax.all_gather(out_grad, 'row', axis=0, tiled=True)]
    reduce_scatter x2 -> x0, waiting for transfers between devices: 124 us -> none  [the longest x1 73.9 us: on_device(): lax.psum_scatter(right_trans(grad_cols, down_weight), 'col', scatter_dime...]
    pallas_call x0 -> x1, Pallas kernels: none -> 106 us  [exchange(): pl.pallas_call(kernel, out_shape=(jax.ShapeDtypeStruct((NK, NJ, TB, dl),...]
    dot_general x3 -> x0, matrix products: 26.4 us -> none  [right_trans(): lax.dot_general(left, right, (((1,), (1,)), ((), ())), preferred_element_...]
    unnamed x8 -> x7, local copies, waits for them, and re-layouts: 13.4 us -> 0.67 us
    convert_element_type x2 -> x0, other arithmetic: 3.8 us -> none  [the longest x1 2.17 us: swiglu_back(): up_delta = (hidden_delta * gate_vals * sigma).astype(jnp.bfloat16)]
  transfers between devices with their start and end apart: 6 -> 0, of which waited for: 6 -> 0; matrix products, arithmetic and copies ran while one was open for 13% -> 0% of each run, Pallas kernels for 0% -> 0%
where the time goes in v1:
time: 124 us; the launch traced here: 122 us
  Pallas kernels  106 us (85%)
  matrix products  14.5 us (12%)
    pallas_call x1, Pallas kernels, exchange(): pl.pallas_call(kernel, out_shape=(jax.ShapeDtypeStruct((NK, NJ, TB, dl),...  106 us
    dot_general x2, matrix products, left_trans(): lax.dot_general(left, right, (((0,), (0,)), ((), ())), preferred_element_...  14.5 us

profile of v1, /device:TPU:1, one launch (start us, length us, event | category | flops | bytes accessed | tf_op | source)
XLA Modules:
  0.0 121.8 jit_solution(9503673836528256810)
XLA Ops:
  0.6 106.0 %shard_map.94 = (bf16[2,3,16,768]{3,2,1,0:T(8,128)(2,1)}, bf16[8,2,3,16,3072]{4,3,2,1,0:T(8,128)(2,1)}, bf16[8,2,3,16,3072]{4,3,2,1,0:T(8,128)(2,1)}, bf16[8,2,3,16,768]{4,3,2,1,0:T(8,128)(2,1)}) custom-call(bf16[2,3,16,768]{3,2,1,0:T(8,128)(2,1)} %bitcast.20, bf16[2,3,16,768]{3,2,1,0:T(8,128)(2,1)} %bitcast.21, bf16[3,16,3072]{2,1,0:T(8,128)(2,1)} %bitcast.18, ...), custom_call_target="tpu_custom_call" | custom-call | flops 10871635968 | bytes 37748736 | tf_op jit(solution)/shard_map/pallas_call | solution.py:388
  106.6 0.0 copy-start.1
  106.6 0.0 copy-start.2
  106.6 8.9 %bitcast_convert_fusion.1 = bf16[768,3072]{1,0:T(8,128)(2,1)} fusion(bf16[8,2,3,16,768]{4,3,2,1,0:T(8,128)(2,1)} %get-tuple-element.8, bf16[8,2,3,16,3072]{4,3,2,1,0:T(8,128)(2,1)} %get-tuple-element.9), kind=kOutput, calls=%fused_computation.1 | convolution fusion | flops 3626237952 | bytes 10616832 | tf_op jit(solution)/shard_map/dot_general | solution.py:24
  115.5 0.0 copy-done.1
  115.6 0.0 copy-done.2
  115.6 0.0 copy-start
  115.6 5.6 %bitcast_convert_fusion = bf16[768,3072]{1,0:T(8,128)(2,1)} fusion(bf16[8,2,3,16,768]{4,3,2,1,0:T(8,128)(2,1)S(1)} %copy-done.2, bf16[8,2,3,16,3072]{4,3,2,1,0:T(8,128)(2,1)S(1)} %copy-done.1), kind=kOutput, calls=%fused_computation | convolution fusion | flops 3626237952 | bytes 10616832 | tf_op jit(solution)/shard_map/dot_general | solution.py:24
  121.1 0.0 copy-done
  121.1 0.7 copy.13
Async XLA Ops:
  106.6 8.9 %copy-start.1 = (bf16[8,2,3,16,3072]{4,3,2,1,0:T(8,128)(2,1)S(1)}, bf16[8,2,3,16,3072]{4,3,2,1,0:T(8,128)(2,1)}, u32[]{:S(2)}) copy-start(bf16[8,2,3,16,3072]{4,3,2,1,0:T(8,128)(2,1)} %get-tuple-element.10) | copy-start | bytes 14155780
  106.6 8.9 %copy-start.2 = (bf16[8,2,3,16,768]{4,3,2,1,0:T(8,128)(2,1)S(1)}, bf16[8,2,3,16,768]{4,3,2,1,0:T(8,128)(2,1)}, u32[]{:S(2)}) copy-start(bf16[8,2,3,16,768]{4,3,2,1,0:T(8,128)(2,1)} %get-tuple-element.8) | copy-start | bytes 3538948
  115.6 5.6 %copy-start = (bf16[2,3,16,768]{3,2,1,0:T(8,128)(2,1)S(1)}, bf16[2,3,16,768]{3,2,1,0:T(8,128)(2,1)}, u32[]{:S(2)}) copy-start(bf16[2,3,16,768]{3,2,1,0:T(8,128)(2,1)} %get-tuple-element.7) | copy-start | bytes 442372

commit v2 on v0

v2 whole, which is shorter than its diff:
```python
import jax
import jax.numpy as jnp
from jax import lax
from jax.experimental import pallas as pl
from jax.experimental.pallas import tpu as pltpu
from jax.sharding import PartitionSpec as P

BF16 = jnp.bfloat16
F32 = jnp.float32
MESH = pl.DeviceIdType.MESH
NY, NZH, NZL, NX, NK = 4, 2, 2, 4, 2
NP = NZL * NX
NJ = 3
TB = 16

UNITS = ((0, 0, 1024), (0, 1024, 1024), (0, 2048, 1024), (1, 0, 1024), (1, 1024, 1024), (1, 2048, 1024), (2, 0, 1024), (2, 1024, 1024), (2, 2048, 1024))
BLOCKS = tuple(sorted({(c0, w) for _, c0, w in UNITS}))
WMAX = max(w for _, w in BLOCKS)

ORDER = (
    ("o0", 0), ("o1", 0), ("o0", 1), ("s0", 0), ("s0", 1), ("o1", 1), ("s0", 2), ("s1", 0),
    ("o0", 2), ("s1", 1), ("s1", 2), ("s0", 3), ("s0", 4), ("s0", 5), ("s1", 3), ("s2", 0),
    ("o1", 2), ("i0", 0), ("s2", 1), ("s3", 0), ("s1", 4), ("s2", 2), ("s0", 6), ("s0", 7),
    ("s3", 1), ("s1", 5), ("s0", 8), ("s2", 3), ("s5", 0), ("s3", 2), ("s1", 6), ("i1", 0),
    ("s5", 1), ("s4", 0), ("s3", 3), ("s7", 0), ("s1", 7), ("s5", 2), ("s2", 4), ("s7", 1),
    ("s4", 1), ("s6", 0), ("s5", 3), ("s7", 2), ("s2", 5), ("s4", 2), ("s3", 4), ("s1", 8),
    ("s6", 1), ("s8", 0), ("s7", 3), ("s2", 6), ("s9", 0), ("s4", 3), ("s3", 5), ("s6", 2),
    ("i2", 0), ("s5", 4), ("s2", 7), ("s8", 1), ("s4", 4), ("s9", 1), ("s3", 6), ("s6", 3),
    ("s2", 8), ("s5", 5), ("s8", 2), ("s4", 5), ("s7", 4), ("s9", 2), ("gs", 0), ("s4", 6),
    ("s3", 7), ("s6", 4), ("s5", 6), ("s8", 3), ("s9", 3), ("s3", 8), ("s7", 5), ("s4", 7),
    ("s6", 5), ("g10", 0), ("s6", 6), ("s4", 8), ("s5", 7), ("s8", 4), ("s7", 6), ("s9", 4),
    ("g11", 0), ("s5", 8), ("s6", 7), ("s8", 5), ("s8", 6), ("s9", 5), ("gs", 1), ("s6", 8),
    ("s9", 6), ("s7", 7), ("s7", 8), ("dw", 0), ("s8", 7), ("dw", 1), ("dw", 2), ("s8", 8),
    ("s9", 7), ("s9", 8), ("gs", 2), ("dw", 3), ("dw", 4), ("g10", 1), ("dw", 5), ("dw", 6),
    ("dw", 7), ("dw", 8), ("dw", 9), ("dw", 10), ("g11", 1), ("dw", 11), ("g11", 2),
)


def right_trans(left, right):
    return lax.dot_general(
        left, right, (((1,), (1,)), ((), ())), preferred_element_type=F32
    )


def kernel(
    og_ref,
    in_ref,
    gp_ref,
    up_ref,
    gw_ref,
    uw_ref,
    dw_ref,
    gi_ref,
    ga_ref,
    ua_ref,
    dwv,
    gwv,
    uwv,
    gpv,
    upv,
    og,
    xg,
    xt,
    db,
    hs,
    hr,
    ho,
    zs,
    zr,
    xs,
    xr,
    gacc,
    gs,
    gr,
    gz,
    gzr,
    load_sem,
    s_og,
    r_og,
    s_in,
    r_in,
    s_rs,
    r_rs,
    s_ag,
    r_ag,
    s_gi,
    r_gi,
):
    r = lax.axis_index("row")
    c = lax.axis_index("col")
    y, zh = r // 2, r % 2
    zl, x, k = c // 8, (c // 2) % 4, c % 2
    p = zl * NX + x
    pz = (1 - zl) * NX + x
    rz = y * 2 + 1 - zh

    def xmod(d):
        return (x + d) % NX

    def ymod(d):
        return (y + d) % NY

    dev_k = (r, c + 1 - 2 * k)
    dev_zl = (r, (1 - zl) * 8 + x * 2 + k)
    dev_zh = (rz, c)

    def dev_x(d):
        return (r, zl * 8 + xmod(d) * 2 + k)

    def dev_y(d, other=False):
        return (ymod(d) * 2 + (1 - zh if other else zh), c)

    dl = dw_ref.shape[1]

    barrier = pltpu.get_barrier_semaphore()
    peers = [dev_k, dev_zl, dev_zh]
    peers += [dev_x(d) for d in (1, 2, 3)]
    peers += [dev_y(d) for d in (1, 2, 3)] + [dev_y(d, True) for d in (1, 2, 3)]
    for dev in peers:
        pl.semaphore_signal(barrier, 1, device_id=dev, device_id_type=MESH)

    loads = {}

    def load(name, src, dst):
        cp = pltpu.make_async_copy(src, dst, load_sem.at[len(loads)])
        cp.start()
        loads[name] = cp

    load("og", og_ref, og.at[r])
    load("dw", dw_ref, dwv)
    load("in", in_ref, xg.at[r])
    load("gp", gp_ref, gpv)
    load("up", up_ref, upv)
    load("gw", gw_ref, gwv)
    load("uw", uw_ref, uwv)
    loaded = set()

    def need(*names):
        for name in names:
            if name not in loaded:
                loaded.add(name)
                loads[name].wait()

    pl.semaphore_wait(barrier, len(peers))

    sent = []
    got = {}

    def send(key, src, dst, ssem, rsem, dev):
        cp = pltpu.make_async_remote_copy(
            src_ref=src,
            dst_ref=dst,
            send_sem=ssem,
            recv_sem=rsem,
            device_id=dev,
            device_id_type=MESH,
        )
        cp.start()
        sent.append(cp)
        got[key] = cp

    def arrived(*keys):
        for key in keys:
            got.pop(key).wait_recv()

    def o0(j):
        src, dst = og_ref.at[:, j], og.at[r, :, j]
        targets = [dev_zh] + [dev_y(d) for d in (1, 3, 2)]
        if j == 0:
            targets += [dev_y(d, True) for d in (1, 3, 2)]
        for n, dev in enumerate(targets):
            send(("og", j, n), src, dst, s_og.at[j, n], r_og.at[j, n], dev)

    def o1(j):
        arrived(("og", j, 0))
        if j == 0:
            return
        ref = og.at[rz, :, j]
        for n, d in enumerate((1, 3, 2)):
            send(("og", j, 4 + n), ref, ref, s_og.at[j, 4 + n], r_og.at[j, 4 + n], dev_y(d))

    def i0(_):
        send(("in", 0), in_ref, xg.at[r], s_in.at[0], r_in.at[0], dev_zh)

    def i1(_):
        need("in")
        arrived(("in", 0))
        ref = xg.at[pl.ds(y * 2, 2)]
        for n, d in enumerate((1, 3, 2)):
            send(("in", 1 + n), ref, ref, s_in.at[1 + n], r_in.at[1 + n], dev_y(d))

    def i2(_):
        arrived(("in", 1), ("in", 2), ("in", 3))
        per = NK * NJ * TB

        def turn(n, _):
            cols = pl.ds(pl.multiple_of(n * 128, 128), 128)
            xt[cols, :] = xg[:, :, :, :, cols].reshape(NP * per, 128).T
            return 0

        lax.fori_loop(0, dl // 128, turn, 0)

    def cols_of(u):
        _, c0, w = UNITS[u]
        return pl.ds(c0, w)

    seen_og = set()

    def s0(u):
        j, c0, w = UNITS[u]
        need("og", "dw")
        if j not in seen_og:
            seen_og.add(j)
            arrived(*[("og", j, n) for n in range(1, 7)])
        left = jnp.concatenate(
            [og[:, 1 - k, j].reshape(NP * TB, dl), og[:, k, j].reshape(NP * TB, dl)], axis=0
        )
        nt = 512

        def tile(n, _):
            rows = pl.ds(pl.multiple_of(c0 + n * nt, nt), nt)
            out = right_trans(left, dwv[rows, :])
            at = pl.ds(pl.multiple_of(n * nt, nt), nt)
            hs[u, :, :, at] = out[: NP * TB].astype(BF16).reshape(NP, TB, nt)
            ho[u, :, :, at] = out[NP * TB :].reshape(NP, TB, nt)
            return 0

        lax.fori_loop(0, w // nt, tile, 0)
        send(("k", u), hs.at[u], hr.at[u], s_rs.at[u, 0], r_rs.at[u, 0], dev_k)

    def s1(u):
        arrived(("k", u))

        def add(i, _):
            far = (1 - zl) * NX + i
            zs[u, i] = (ho[u, far] + hr[u, far].astype(F32)).astype(BF16)
            return 0

        lax.fori_loop(0, NX, add, 0)
        send(("z", u), zs.at[u], zr.at[u], s_rs.at[u, 1], r_rs.at[u, 1], dev_zl)

    def s2(u):
        arrived(("z", u))
        for d in (1, 3, 2):
            q = xmod(d)
            near = zl * NX + q
            xs[u, d - 1] = (
                ho[u, near] + hr[u, near].astype(F32) + zr[u, q].astype(F32)
            ).astype(BF16)
            send(
                ("x", u, d),
                xs.at[u, d - 1],
                xr.at[u, d - 1],
                s_rs.at[u, 1 + d],
                r_rs.at[u, 1 + d],
                dev_x(d),
            )

    def piece(u, q):
        return db.at[:, q, k, UNITS[u][0], :, cols_of(u)]

    def part(u, a, q):
        return db.at[a, q, k, UNITS[u][0], :, cols_of(u)]

    def ag_send(u, n, ref, dev):
        send(("a", u, n), ref, ref, s_ag.at[u, n], r_ag.at[u, n], dev)

    def s3(u):
        need("gp", "up")
        arrived(("x", u, 1), ("x", u, 3), ("x", u, 2))
        j = UNITS[u][0]
        cols = cols_of(u)
        hidden = ho[u, p] + hr[u, p].astype(F32) + zr[u, x].astype(F32)
        for d in (1, 2, 3):
            hidden = hidden + xr[u, d - 1].astype(F32)
        g = gpv[j, :, cols].astype(F32)
        up = upv[j, :, cols].astype(F32)
        s = jax.nn.sigmoid(g)
        db[1, p, k, j, :, cols] = (hidden * g * s).astype(BF16)
        db[0, p, k, j, :, cols] = (hidden * up * s * (1.0 + g * (1.0 - s))).astype(BF16)
        ref = piece(u, p)
        ag_send(u, 0, ref, dev_zl)
        ag_send(u, 1, ref, dev_x(1))
        ag_send(u, 2, ref, dev_x(3))
        ag_send(u, 3, ref, dev_k)

    def s4(u):
        arrived(("a", u, 0))
        ref = piece(u, pz)
        ag_send(u, 4, ref, dev_x(1))
        ag_send(u, 5, ref, dev_x(3))
        ag_send(u, 6, ref, dev_k)

    def relay(u, first, base, lane):
        lo = lane * NX + xmod(3)
        hi = lane * NX + xmod(1)
        arrived(("a", u, first))
        ag_send(u, base, part(u, 0, lo), dev_x(1))
        arrived(("a", u, first + 1))
        ag_send(u, base + 1, part(u, 1, hi), dev_x(3))
        ag_send(u, base + 2, piece(u, lo), dev_k)
        ag_send(u, base + 3, piece(u, hi), dev_k)

    def s5(u):
        relay(u, 1, 7, zl)

    def s6(u):
        relay(u, 4, 11, 1 - zl)

    def s7(u):
        arrived(("a", u, 7), ("a", u, 8))
        ag_send(u, 15, piece(u, zl * NX + xmod(2)), dev_k)

    def s8(u):
        arrived(("a", u, 11), ("a", u, 12))
        ag_send(u, 16, piece(u, (1 - zl) * NX + xmod(2)), dev_k)

    begun = set()

    def s9(u):
        j, c0, w = UNITS[u]
        cols = cols_of(u)
        need("gw", "uw")
        arrived(*[("a", u, n) for n in (3, 6, 9, 10, 13, 14, 15, 16)])
        dgate = db[0, :, :, j, :, cols].reshape(NP * NK * TB, w)
        dup = db[1, :, :, j, :, cols].reshape(NP * NK * TB, w)
        out = right_trans(dgate, gwv[:, cols]) + right_trans(dup, uwv[:, cols])
        if j in begun:
            out = out + gacc[j]
        begun.add(j)
        gacc[j] = out

    def gs0(j):
        gs[j] = gacc[j].astype(BF16).reshape(NP, NK, TB, dl)
        for d in (1, 3, 2):
            q = ymod(d)
            if j < NJ - 1:
                send(
                    ("g", j, d),
                    gs.at[j, pl.ds(q * 2, 2)],
                    gr.at[j, d - 1],
                    s_gi.at[j, d],
                    r_gi.at[j, d],
                    dev_y(d),
                )
            else:
                for e in (0, 1):
                    dest = q * 2 + (zh if e == 0 else 1 - zh)
                    send(
                        ("g", j, d + 3 * e),
                        gs.at[j, dest],
                        gr.at[j, d - 1, e],
                        s_gi.at[j, d + 3 * e],
                        r_gi.at[j, d + 3 * e],
                        dev_y(d, e == 1),
                    )
        if j == NJ - 1:
            send(("g", j, 0), gs.at[j, rz], gzr.at[j], s_gi.at[j, 0], r_gi.at[j, 0], dev_zh)

    def rows_of(dest):
        return pl.ds(pl.multiple_of(dest * NK * TB, NK * TB), NK * TB)

    def g10(j):
        arrived(("g", j, 1), ("g", j, 3), ("g", j, 2))

        def total(q):
            acc = gacc[j, rows_of(y * 2 + q), :].reshape(NK, TB, dl)
            for d in (1, 2, 3):
                acc = acc + gr[j, d - 1, q].astype(F32)
            return acc

        gz[j] = total(1 - zh).astype(BF16)
        send(("g", j, 0), gz.at[j], gzr.at[j], s_gi.at[j, 0], r_gi.at[j, 0], dev_zh)
        own = total(zh).reshape(NK * TB, dl)
        gacc[j, rows_of(r), :] = own

    def g11(j):
        if j == NJ - 1:
            arrived(*[("g", j, n) for n in range(1, 7)])
        arrived(("g", j, 0))
        acc = gacc[j, rows_of(r), :].reshape(NK, TB, dl) + gzr[j].astype(F32)
        if j == NJ - 1:
            for d in (1, 2, 3):
                for e in (0, 1):
                    acc = acc + gr[j, d - 1, e].astype(F32)
        gi_ref[:, j] = acc.astype(BF16)

    def dw(n):
        c0, w = BLOCKS[n // 4]
        a, half = n % 4 // 2, n % 2
        cols = pl.ds(c0 + half * (w // 2), w // 2)
        right = db[a, :, :, :, :, cols].reshape(NP * NK * NJ * TB, w // 2)
        out = jnp.dot(xt[...], right, preferred_element_type=F32)
        (ga_ref, ua_ref)[a][:, cols] = out.astype(BF16)

    steps = dict(
        o0=o0, o1=o1, i0=i0, i1=i1, i2=i2, s0=s0, s1=s1, s2=s2, s3=s3, s4=s4, s5=s5, s6=s6,
        s7=s7, s8=s8, s9=s9, gs=gs0, g10=g10, g11=g11, dw=dw,
    )
    for name, arg in ORDER:
        steps[name](arg)
    for cp in sent:
        cp.wait_send()


def on_device(inputs, out_grad, gate_pre, up_pre, gate_weight, up_weight, down_weight):
    ff, dl = down_weight.shape
    nu = len(UNITS)
    tok = NP * NK * NJ * TB
    dma = pltpu.SemaphoreType.DMA
    vm = pltpu.VMEM
    hbm = pl.BlockSpec(memory_space=pl.ANY)
    whole = pl.BlockSpec(memory_space=pltpu.VMEM)
    grad_input, grad_gate, grad_up = pl.pallas_call(
        kernel,
        out_shape=(
            jax.ShapeDtypeStruct((NK, NJ, TB, dl), BF16),
            pltpu.VMEM((dl, ff), BF16),
            pltpu.VMEM((dl, ff), BF16),
        ),
        in_specs=[hbm] * 7,
        out_specs=(whole, whole, whole),
        scratch_shapes=[
            vm((ff, dl), BF16),
            vm((dl, ff), BF16),
            vm((dl, ff), BF16),
            vm((NJ, TB, ff), BF16),
            vm((NJ, TB, ff), BF16),
            vm((NP, NK, NJ, TB, dl), BF16),
            vm((NP, NK, NJ, TB, dl), BF16),
            vm((dl, tok), BF16),
            vm((2, NP, NK, NJ, TB, ff), BF16),
            vm((nu, NP, TB, WMAX), BF16),
            vm((nu, NP, TB, WMAX), BF16),
            vm((nu, NP, TB, WMAX), F32),
            vm((nu, NX, TB, WMAX), BF16),
            vm((nu, NX, TB, WMAX), BF16),
            vm((nu, 3, TB, WMAX), BF16),
            vm((nu, 3, TB, WMAX), BF16),
            vm((NJ, NP * NK * TB, dl), F32),
            vm((NJ, NP, NK, TB, dl), BF16),
            vm((NJ, 3, 2, NK, TB, dl), BF16),
            vm((NJ, NK, TB, dl), BF16),
            vm((NJ, NK, TB, dl), BF16),
            dma((7,)),
            dma((NJ, 7)),
            dma((NJ, 7)),
            dma((4,)),
            dma((4,)),
            dma((nu, 5)),
            dma((nu, 5)),
            dma((nu, 17)),
            dma((nu, 17)),
            dma((NJ, 7)),
            dma((NJ, 7)),
        ],
        compiler_params=pltpu.CompilerParams(
            collective_id=0, has_side_effects=True, vmem_limit_bytes=51 * 2**20
        ),
        cost_estimate=pl.CostEstimate(
            flops=10 * tok * dl * ff, bytes_accessed=10 * dl * ff, transcendentals=0
        ),
    )(
        out_grad.reshape(NK, NJ, TB, dl),
        inputs.reshape(NK, NJ, TB, dl),
        gate_pre.reshape(NJ, TB, ff),
        up_pre.reshape(NJ, TB, ff),
        gate_weight,
        up_weight,
        down_weight,
    )
    return (grad_input.reshape(NK * NJ * TB, dl), grad_gate, grad_up)


def solution(mesh):
    placed = (
        P("row", "col"),
        P("row", "col"),
        P("col", "row"),
        P("col", "row"),
        P("col", "row"),
        P("col", "row"),
        P("row", "col"),
    )
    return jax.shard_map(
        on_device,
        mesh=mesh,
        in_specs=placed,
        out_specs=(P("row", "col"), P("col", "row"), P("col", "row")),
        check_vma=False,
    )
```

time: 366 us -> 105 us (0.29)
  waiting for transfers between devices: 290 us -> 0 us
  Pallas kernels: 0 us -> 99 us
  matrix products: 43.2 us -> 0 us
  between operations: 14.1 us -> 0.64 us
  local copies, waits for them, and re-layouts: 13.4 us -> 5.04 us
  other arithmetic: 3.8 us -> 0 us
    all_gather x4 -> x0, waiting for transfers between devices: 165 us -> none  [the longest x1 52.5 us: on_device(): lax.all_gather(out_grad, 'row', axis=0, tiled=True)]
    reduce_scatter x2 -> x0, waiting for transfers between devices: 124 us -> none  [the longest x1 73.9 us: on_device(): lax.psum_scatter(right_trans(grad_cols, down_weight), 'col', scatter_dime...]
    pallas_call x0 -> x1, Pallas kernels: none -> 99 us  [on_device(): pl.pallas_call(kernel, out_shape=(jax.ShapeDtypeStruct((NK, NJ, TB, dl),...]
    dot_general x5 -> x0, matrix products: 43.2 us -> none  [the longest x3 26.4 us: right_trans(): lax.dot_general(left, right, (((1,), (1,)), ((), ())), preferred_element_...]
    unnamed x8 -> x5, local copies, waits for them, and re-layouts: 13.4 us -> 5.04 us
    convert_element_type x2 -> x0, other arithmetic: 3.8 us -> none  [the longest x1 2.17 us: swiglu_back(): up_delta = (hidden_delta * gate_vals * sigma).astype(jnp.bfloat16)]
  transfers between devices with their start and end apart: 6 -> 0, of which waited for: 6 -> 0; matrix products, arithmetic and copies ran while one was open for 13% -> 0% of each run, Pallas kernels for 0% -> 0%
where the time goes in v2:
time: 105 us
  Pallas kernels  99 us (94%)
  local copies, waits for them, and re-layouts  5.04 us (5%)
    pallas_call x1, Pallas kernels, on_device(): pl.pallas_call(kernel, out_shape=(jax.ShapeDtypeStruct((NK, NJ, TB, dl),...  99 us
    unnamed x5, local copies, waits for them, and re-layouts  5.04 us

profile of v2, /device:TPU:1, one launch (start us, length us, event | category | flops | bytes accessed | tf_op | source)
XLA Modules:
  0.0 104.7 jit_solution(15361983910941250005)
XLA Ops:
  0.6 99.0 %shard_map.94 = (bf16[2,3,16,768]{3,2,1,0:T(8,128)(2,1)}, bf16[768,3072]{1,0:T(8,128)(2,1)S(1)}, bf16[768,3072]{1,0:T(8,128)(2,1)S(1)}) custom-call(bf16[2,3,16,768]{3,2,1,0:T(8,128)(2,1)} %bitcast.8, bf16[2,3,16,768]{3,2,1,0:T(8,128)(2,1)} %bitcast.9, bf16[3,16,3072]{2,1,0:T(8,128)(2,1)} %bitcast.6, bf16[3,16,3072]{2,1,0:T(8,128)(2,1)} %bitcast.7, ...), custom_call_target="tpu_custom_call" | custom-call | flops 18119393280 | bytes 23592960 | tf_op jit(solution)/shard_map/pallas_call | solution.py:414
  99.6 2.2 %copy.13 = bf16[768,3072]{1,0:T(8,128)(2,1)} copy(bf16[768,3072]{1,0:T(8,128)(2,1)S(1)} %get-tuple-element.10) | data formatting | bytes 9437184
  101.8 0.0 copy-start
  101.8 2.2 %copy.14 = bf16[768,3072]{1,0:T(8,128)(2,1)} copy(bf16[768,3072]{1,0:T(8,128)(2,1)S(1)} %get-tuple-element.11) | data formatting | bytes 9437184
  104.0 0.0 copy-done
  104.0 0.7 copy.15
Async XLA Ops:
  101.8 2.2 %copy-start = (bf16[2,3,16,768]{3,2,1,0:T(8,128)(2,1)S(1)}, bf16[2,3,16,768]{3,2,1,0:T(8,128)(2,1)}, u32[]{:S(2)}) copy-start(bf16[2,3,16,768]{3,2,1,0:T(8,128)(2,1)} %get-tuple-element.6) | copy-start | bytes 442372

commit v3 on v2

v3 whole, which is shorter than its diff:
```python
import jax
import jax.numpy as jnp
from jax import lax
from jax.experimental import pallas as pl
from jax.experimental.pallas import tpu as pltpu
from jax.sharding import PartitionSpec as P

BF16 = jnp.bfloat16
F32 = jnp.float32
MESH = pl.DeviceIdType.MESH
NY, NZH, NZL, NX, NK = 4, 2, 2, 4, 2
NP = NZL * NX
NJ = 3
TB = 16

UNITS = ((0, 2048, 1024), (0, 0, 1024), (0, 1024, 1024), (1, 0, 1024), (1, 2048, 1024), (1, 1024, 1024), (2, 0, 1024), (2, 1024, 1024), (2, 2048, 1024))
SUM_X_FIRST = (4, 3, 6, 2, 0)
GATHER_X_FIRST = (1, 0, 7, 5)
DIRECT_FIRST = False
BLOCKS = tuple(sorted({(c0, w) for _, c0, w in UNITS}))
WMAX = max(w for _, w in BLOCKS)

ORDER = (
    ("o0", 0), ("o1", 0), ("o0", 1), ("o1", 1), ("o0", 2), ("s0", 0), ("s0", 1), ("s0", 2),
    ("s1", 0), ("s1", 1), ("o1", 2), ("i0", 0), ("s1", 2), ("s0", 3), ("s0", 4), ("s0", 5),
    ("s1", 3), ("s1", 4), ("s1", 5), ("s2", 1), ("s2", 0), ("s0", 6), ("s0", 7), ("s0", 8),
    ("s1", 6), ("s2", 2), ("s1", 7), ("i1", 0), ("s1", 8), ("s2", 3), ("s2", 5), ("s3", 0),
    ("s3", 2), ("s2", 4), ("s3", 1), ("s2", 7), ("s2", 6), ("s2", 8), ("s3", 3), ("s3", 5),
    ("s5", 0), ("s4", 0), ("s5", 2), ("s4", 2), ("s3", 4), ("s5", 1), ("s4", 1), ("s3", 6),
    ("i2", 0), ("s3", 7), ("s4", 3), ("s3", 8), ("s5", 3), ("s4", 5), ("s5", 5), ("s7", 0),
    ("s7", 2), ("s6", 0), ("s6", 2), ("s4", 4), ("s5", 4), ("s7", 1), ("s6", 1), ("s5", 6),
    ("s4", 6), ("s5", 7), ("s4", 7), ("s6", 3), ("s4", 8), ("s5", 8), ("s7", 3), ("s7", 5),
    ("s8", 2), ("s6", 5), ("s9", 2), ("s6", 4), ("s7", 4), ("s8", 0), ("s7", 6), ("s8", 1),
    ("s9", 0), ("s6", 6), ("s9", 1), ("gs", 0), ("s6", 7), ("s7", 7), ("s8", 3), ("s6", 8),
    ("s8", 5), ("s9", 3), ("s7", 8), ("s8", 4), ("s9", 5), ("s8", 6), ("s9", 4), ("gs", 1),
    ("s8", 7), ("s8", 8), ("s9", 6), ("s9", 7), ("s9", 8), ("gs", 2), ("g10", 0), ("dw", 0),
    ("dw", 1), ("dw", 2), ("g10", 1), ("dw", 3), ("g11", 0), ("dw", 4), ("g11", 2), ("dw", 5),
    ("g11", 1),
)


def right_trans(left, right):
    return lax.dot_general(
        left, right, (((1,), (1,)), ((), ())), preferred_element_type=F32
    )


def kernel(
    og_ref,
    in_ref,
    gp_ref,
    up_ref,
    gw_ref,
    uw_ref,
    dw_ref,
    gi_ref,
    ga_ref,
    ua_ref,
    dwv,
    gwv,
    uwv,
    gpv,
    upv,
    og,
    xg,
    xt,
    db,
    hs,
    hr,
    ho,
    zs,
    zr,
    xs,
    xr,
    gacc,
    gs,
    gr,
    gz,
    gzr,
    load_sem,
    send_sem,
    r_og,
    r_in,
    r_rs,
    r_ag,
    r_gi,
):
    r = lax.axis_index("row")
    c = lax.axis_index("col")
    y, zh = r // 2, r % 2
    zl, x, k = c // 8, (c // 2) % 4, c % 2
    p = zl * NX + x
    pz = (1 - zl) * NX + x
    rz = y * 2 + 1 - zh

    def xmod(d):
        return (x + d) % NX

    def ymod(d):
        return (y + d) % NY

    dev_k = (r, c + 1 - 2 * k)
    dev_zl = (r, (1 - zl) * 8 + x * 2 + k)
    dev_zh = (rz, c)

    def dev_x(d):
        return (r, zl * 8 + xmod(d) * 2 + k)

    def dev_y(d, other=False):
        return (ymod(d) * 2 + (1 - zh if other else zh), c)

    dl = dw_ref.shape[1]

    barrier = pltpu.get_barrier_semaphore()
    peers = [dev_k, dev_zl, dev_zh]
    peers += [dev_x(d) for d in (1, 2, 3)]
    peers += [dev_y(d) for d in (1, 2, 3)]
    if DIRECT_FIRST:
        peers += [dev_y(d, True) for d in (1, 2, 3)]
    for dev in peers:
        pl.semaphore_signal(barrier, 1, device_id=dev, device_id_type=MESH)

    loads = {}

    def load(name, src, dst):
        cp = pltpu.make_async_copy(src, dst, load_sem.at[len(loads)])
        cp.start()
        loads[name] = cp

    load("og", og_ref, og.at[r])
    load("dw", dw_ref, dwv)
    load("in", in_ref, xg.at[r])
    load("gp", gp_ref, gpv)
    load("up", up_ref, upv)
    load("gw", gw_ref, gwv)
    load("uw", uw_ref, uwv)
    loaded = set()

    def need(*names):
        for name in names:
            if name not in loaded:
                loaded.add(name)
                loads[name].wait()

    pl.semaphore_wait(barrier, len(peers))

    def send(src, dst, ssem, rsem, dev):
        pltpu.make_async_remote_copy(
            src_ref=src,
            dst_ref=dst,
            send_sem=send_sem.at[ssem],
            recv_sem=rsem,
            device_id=dev,
            device_id_type=MESH,
        ).start()

    def arrived(ref, sem):
        pltpu.make_async_copy(ref, ref, sem).wait()

    def o0(j):
        src, dst = og_ref.at[:, j], og.at[r, :, j]
        send(src, dst, 0, r_og.at[j, 0], dev_zh)
        for d in (1, 3, 2):
            send(src, dst, 0, r_og.at[j, 1], dev_y(d))
        if j == 0 and DIRECT_FIRST:
            for d in (1, 3, 2):
                send(src, dst, 0, r_og.at[j, 1], dev_y(d, True))

    def o1(j):
        arrived(og.at[0, :, j], r_og.at[j, 0])
        if j > 0 or not DIRECT_FIRST:
            ref = og.at[rz, :, j]
            for d in (1, 3, 2):
                send(ref, ref, 0, r_og.at[j, 1], dev_y(d))

    def i0(_):
        send(in_ref, xg.at[r], 1, r_in.at[0], dev_zh)

    def i1(_):
        need("in")
        arrived(xg.at[0], r_in.at[0])
        ref = xg.at[pl.ds(y * 2, 2)]
        for d in (1, 3, 2):
            send(ref, ref, 1, r_in.at[1], dev_y(d))

    def i2(_):
        arrived(xg.at[pl.ds(0, 6)], r_in.at[1])
        per = NK * NJ * TB

        def turn(n, _):
            cols = pl.ds(pl.multiple_of(n * 128, 128), 128)
            xt[cols, :] = xg[:, :, :, :, cols].reshape(NP * per, 128).T
            return 0

        lax.fori_loop(0, dl // 128, turn, 0)

    def cols_of(u):
        _, c0, w = UNITS[u]
        return pl.ds(c0, w)

    seen_og = set()

    def s0(u):
        j, c0, w = UNITS[u]
        need("og", "dw")
        if j not in seen_og:
            seen_og.add(j)
            arrived(og.at[pl.ds(0, 6), :, j], r_og.at[j, 1])
        left = jnp.concatenate(
            [og[:, 1 - k, j].reshape(NP * TB, dl), og[:, k, j].reshape(NP * TB, dl)], axis=0
        )
        nt = 768 if w % 768 == 0 else 512

        def tile(n, _):
            rows = pl.ds(pl.multiple_of(c0 + n * nt, nt), nt)
            out = right_trans(left, dwv[rows, :])
            at = pl.ds(pl.multiple_of(n * nt, nt), nt)
            hs[u, :, :, at] = out[: NP * TB].astype(BF16).reshape(NP, TB, nt)
            ho[u, :, :, at] = out[NP * TB :].reshape(NP, TB, nt)
            return 0

        lax.fori_loop(0, w // nt, tile, 0)
        send(hs.at[u], hr.at[u], 3 + j, r_rs.at[u, 0], dev_k)

    def core_sum(u, q):
        return ho[u, q] + hr[u, q].astype(F32)

    def s1(u):
        j = UNITS[u][0]
        arrived(hr.at[u], r_rs.at[u, 0])
        if u in SUM_X_FIRST:
            for d in (1, 3, 2):
                for lane in range(NZL):
                    xs[u, d - 1, lane] = core_sum(u, lane * NX + xmod(d)).astype(BF16)
                send(xs.at[u, d - 1], xr.at[u, d - 1], 3 + j, r_rs.at[u, 1], dev_x(d))
        else:

            def add(i, _):
                zs[u, i] = core_sum(u, (1 - zl) * NX + i).astype(BF16)
                return 0

            lax.fori_loop(0, NX, add, 0)
            send(zs.at[u], zr.at[u], 3 + j, r_rs.at[u, 1], dev_zl)

    def s2(u):
        j = UNITS[u][0]
        if u in SUM_X_FIRST:
            arrived(xr.at[u], r_rs.at[u, 1])
            total = core_sum(u, pz)
            for d in (1, 2, 3):
                total = total + xr[u, d - 1, 1 - zl].astype(F32)
            zs[u, 0] = total.astype(BF16)
            send(zs.at[u, 0], zr.at[u, 0], 3 + j, r_rs.at[u, 2], dev_zl)
        else:
            arrived(zr.at[u], r_rs.at[u, 1])
            for d in (1, 3, 2):
                q = xmod(d)
                xs[u, d - 1, 0] = (core_sum(u, zl * NX + q) + zr[u, q].astype(F32)).astype(BF16)
                send(xs.at[u, d - 1, 0], xr.at[u, d - 1, 0], 3 + j, r_rs.at[u, 2], dev_x(d))

    def piece(u, q):
        return db.at[:, q, k, UNITS[u][0], :, cols_of(u)]

    def pieces(u, n):
        return db.at[:, pl.ds(0, n), 0, UNITS[u][0], :, cols_of(u)]

    def part(u, a, q):
        return db.at[a, q, k, UNITS[u][0], :, cols_of(u)]

    def ag_send(u, n, ref, dev):
        send(ref, ref, 3 + NJ + UNITS[u][0], r_ag.at[u, n], dev)

    def s3(u):
        need("gp", "up")
        j = UNITS[u][0]
        cols = cols_of(u)
        if u in SUM_X_FIRST:
            arrived(zr.at[u, 0], r_rs.at[u, 2])
            hidden = core_sum(u, p) + zr[u, 0].astype(F32)
            lane = zl
        else:
            arrived(xr.at[u, :, 0], r_rs.at[u, 2])
            hidden = core_sum(u, p) + zr[u, x].astype(F32)
            lane = 0
        for d in (1, 2, 3):
            hidden = hidden + xr[u, d - 1, lane].astype(F32)
        g = gpv[j, :, cols].astype(F32)
        up = upv[j, :, cols].astype(F32)
        s = jax.nn.sigmoid(g)
        db[1, p, k, j, :, cols] = (hidden * g * s).astype(BF16)
        db[0, p, k, j, :, cols] = (hidden * up * s * (1.0 + g * (1.0 - s))).astype(BF16)
        ref = piece(u, p)
        ag_send(u, 1, ref, dev_x(1))
        ag_send(u, 1, ref, dev_x(3))
        ag_send(u, 0, ref, dev_zl)
        ag_send(u, 5, ref, dev_k)

    def s4(u):
        arrived(pieces(u, 1), r_ag.at[u, 0])
        ref = piece(u, pz)
        if u not in GATHER_X_FIRST:
            ag_send(u, 2, ref, dev_x(1))
            ag_send(u, 2, ref, dev_x(3))
        ag_send(u, 5, ref, dev_k)

    def sides(u, first, then, lane, relay):
        lo = lane * NX + xmod(3)
        hi = lane * NX + xmod(1)
        arrived(pieces(u, 2), r_ag.at[u, first])
        if relay:
            ag_send(u, then, part(u, 0, lo), dev_x(1))
            ag_send(u, then, part(u, 1, hi), dev_x(3))
        if relay and u in GATHER_X_FIRST:
            ag_send(u, 2, piece(u, lo), dev_zl)
            ag_send(u, 2, piece(u, hi), dev_zl)
        ag_send(u, 5, piece(u, lo), dev_k)
        ag_send(u, 5, piece(u, hi), dev_k)

    def s5(u):
        sides(u, 1, 3, zl, True)

    def s6(u):
        sides(u, 2, 4, 1 - zl, u not in GATHER_X_FIRST)

    def s7(u):
        arrived(pieces(u, 1), r_ag.at[u, 3])
        ref = piece(u, zl * NX + xmod(2))
        if u in GATHER_X_FIRST:
            ag_send(u, 4, ref, dev_zl)
        ag_send(u, 5, ref, dev_k)

    def s8(u):
        arrived(pieces(u, 1), r_ag.at[u, 4])
        ag_send(u, 5, piece(u, (1 - zl) * NX + xmod(2)), dev_k)

    begun = set()

    def s9(u):
        j, c0, w = UNITS[u]
        cols = cols_of(u)
        need("gw", "uw")
        arrived(pieces(u, NP), r_ag.at[u, 5])
        dgate = db[0, :, :, j, :, cols].reshape(NP * NK * TB, w)
        dup = db[1, :, :, j, :, cols].reshape(NP * NK * TB, w)
        out = right_trans(dgate, gwv[:, cols]) + right_trans(dup, uwv[:, cols])
        if j in begun:
            out = out + gacc[j]
        begun.add(j)
        gacc[j] = out

    def gs0(j):
        gs[j] = gacc[j].astype(BF16).reshape(NP, NK, TB, dl)
        for d in (1, 3, 2):
            q = ymod(d) * 2
            if j < NJ - 1:
                send(gs.at[j, pl.ds(q, 2)], gr.at[j, d - 1], 2, r_gi.at[j, 1], dev_y(d))
            else:
                send(gs.at[j, q + zh], gr.at[j, d - 1, 0], 2, r_gi.at[j, 1], dev_y(d))
                send(gs.at[j, q + 1 - zh], gr.at[j, d - 1, 1], 2, r_gi.at[j, 1], dev_y(d, True))
        if j == NJ - 1:
            send(gs.at[j, rz], gzr.at[j], 2, r_gi.at[j, 0], dev_zh)

    def rows_of(dest):
        return pl.ds(pl.multiple_of(dest * NK * TB, NK * TB), NK * TB)

    def g10(j):
        arrived(gr.at[j], r_gi.at[j, 1])

        def total(q):
            acc = gacc[j, rows_of(y * 2 + q), :].reshape(NK, TB, dl)
            for d in (1, 2, 3):
                acc = acc + gr[j, d - 1, q].astype(F32)
            return acc

        gz[j] = total(1 - zh).astype(BF16)
        send(gz.at[j], gzr.at[j], 2, r_gi.at[j, 0], dev_zh)
        gacc[j, rows_of(r), :] = total(zh).reshape(NK * TB, dl)

    def g11(j):
        arrived(gzr.at[j], r_gi.at[j, 0])
        acc = gacc[j, rows_of(r), :].reshape(NK, TB, dl) + gzr[j].astype(F32)
        if j == NJ - 1:
            arrived(gr.at[j], r_gi.at[j, 1])
            for d in (1, 2, 3):
                for e in (0, 1):
                    acc = acc + gr[j, d - 1, e].astype(F32)
        gi_ref[:, j] = acc.astype(BF16)

    def dw(n):
        c0, w = BLOCKS[n // 2]
        cols = pl.ds(c0, w)
        right = db[n % 2, :, :, :, :, cols].reshape(NP * NK * NJ * TB, w)
        out = jnp.dot(xt[...], right, preferred_element_type=F32)
        (ga_ref, ua_ref)[n % 2][:, cols] = out.astype(BF16)

    steps = dict(
        o0=o0, o1=o1, i0=i0, i1=i1, i2=i2, s0=s0, s1=s1, s2=s2, s3=s3, s4=s4, s5=s5, s6=s6,
        s7=s7, s8=s8, s9=s9, gs=gs0, g10=g10, g11=g11, dw=dw,
    )
    for name, arg in ORDER:
        steps[name](arg)
    for n in range(3):
        arrived(og.at[pl.ds(0, 7)], send_sem.at[n])
    for j in range(NJ):
        arrived(db.at[0, pl.ds(0, 5), 0], send_sem.at[3 + j])
        arrived(db.at[:, pl.ds(0, 5), 0], send_sem.at[3 + NJ + j])


def store(gi, ga, ua, gi_out, ga_out, ua_out, sem):
    half = ga.shape[0] // 2
    top, low = pl.ds(0, half), pl.ds(half, half)
    copies = [(gi, gi_out)]
    for src, dst in ((ga, ga_out), (ua, ua_out)):
        copies += [(src.at[top], dst.at[top]), (src.at[low], dst.at[low])]
    started = []
    for n, (src, dst) in enumerate(copies):
        cp = pltpu.make_async_copy(src, dst, sem.at[n])
        cp.start()
        started.append(cp)
    for cp in started:
        cp.wait()


def on_device(inputs, out_grad, gate_pre, up_pre, gate_weight, up_weight, down_weight):
    ff, dl = down_weight.shape
    nu = len(UNITS)
    tok = NP * NK * NJ * TB
    dma = pltpu.SemaphoreType.DMA
    vm = pltpu.VMEM
    hbm = pl.BlockSpec(memory_space=pl.ANY)
    whole = pl.BlockSpec(memory_space=pltpu.VMEM)
    grad_input, grad_gate, grad_up = pl.pallas_call(
        kernel,
        out_shape=(
            pltpu.VMEM((NK, NJ, TB, dl), BF16),
            pltpu.VMEM((dl, ff), BF16),
            pltpu.VMEM((dl, ff), BF16),
        ),
        in_specs=[hbm] * 7,
        out_specs=(whole, whole, whole),
        scratch_shapes=[
            vm((ff, dl), BF16),
            vm((dl, ff), BF16),
            vm((dl, ff), BF16),
            vm((NJ, TB, ff), BF16),
            vm((NJ, TB, ff), BF16),
            vm((NP, NK, NJ, TB, dl), BF16),
            vm((NP, NK, NJ, TB, dl), BF16),
            vm((dl, tok), BF16),
            vm((2, NP, NK, NJ, TB, ff), BF16),
            vm((nu, NP, TB, WMAX), BF16),
            vm((nu, NP, TB, WMAX), BF16),
            vm((nu, NP, TB, WMAX), F32),
            vm((nu, NX, TB, WMAX), BF16),
            vm((nu, NX, TB, WMAX), BF16),
            vm((nu, 3, NZL, TB, WMAX), BF16),
            vm((nu, 3, NZL, TB, WMAX), BF16),
            vm((NJ, NP * NK * TB, dl), F32),
            vm((NJ, NP, NK, TB, dl), BF16),
            vm((NJ, 3, 2, NK, TB, dl), BF16),
            vm((NJ, NK, TB, dl), BF16),
            vm((NJ, NK, TB, dl), BF16),
            dma((7,)),
            dma((3 + 2 * NJ,)),
            dma((NJ, 2)),
            dma((2,)),
            dma((nu, 3)),
            dma((nu, 6)),
            dma((NJ, 2)),
        ],
        compiler_params=pltpu.CompilerParams(
            collective_id=0, has_side_effects=True, vmem_limit_bytes=48 * 2**20
        ),
        cost_estimate=pl.CostEstimate(
            flops=10 * tok * dl * ff, bytes_accessed=10 * dl * ff, transcendentals=0
        ),
    )(
        out_grad.reshape(NK, NJ, TB, dl),
        inputs.reshape(NK, NJ, TB, dl),
        gate_pre.reshape(NJ, TB, ff),
        up_pre.reshape(NJ, TB, ff),
        gate_weight,
        up_weight,
        down_weight,
    )
    grad_input, grad_gate, grad_up = pl.pallas_call(
        store,
        out_shape=(
            jax.ShapeDtypeStruct((NK, NJ, TB, dl), BF16),
            jax.ShapeDtypeStruct((dl, ff), BF16),
            jax.ShapeDtypeStruct((dl, ff), BF16),
        ),
        in_specs=[whole] * 3,
        out_specs=(hbm, hbm, hbm),
        scratch_shapes=[dma((5,))],
        compiler_params=pltpu.CompilerParams(vmem_limit_bytes=4 * 2**20),
    )(*(pltpu.with_memory_space_constraint(a, pltpu.VMEM) for a in (grad_input, grad_gate, grad_up)))
    return (grad_input.reshape(NK * NJ * TB, dl), grad_gate, grad_up)


def solution(mesh):
    placed = (
        P("row", "col"),
        P("row", "col"),
        P("col", "row"),
        P("col", "row"),
        P("col", "row"),
        P("col", "row"),
        P("row", "col"),
    )
    return jax.shard_map(
        on_device,
        mesh=mesh,
        in_specs=placed,
        out_specs=(P("row", "col"), P("col", "row"), P("col", "row")),
        check_vma=False,
    )
```

time: 105 us -> 93.9 us (0.89)
  Pallas kernels: 99 us -> 92.9 us
  local copies, waits for them, and re-layouts: 5.04 us -> 0 us
    pallas_call x1 -> x2, Pallas kernels: 99 us -> 92.9 us  [the longest x1 89.2 us: on_device(): pl.pallas_call(kernel, out_shape=(pltpu.VMEM((NK, NJ, TB, dl), BF16), plt...]
    unnamed x5 -> x0, local copies, waits for them, and re-layouts: 5.04 us -> none
where the time goes in v3:
time: 93.9 us; the launch traced here: 93.8 us
  Pallas kernels  92.9 us (99%)
    pallas_call x1, Pallas kernels, on_device(): pl.pallas_call(kernel, out_shape=(pltpu.VMEM((NK, NJ, TB, dl), BF16), plt...  89.2 us
    pallas_call x1, Pallas kernels, on_device(): pl.pallas_call(store, out_shape=(jax.ShapeDtypeStruct((NK, NJ, TB, dl), B...  3.76 us

profile of v3, /device:TPU:1, one launch (start us, length us, event | category | flops | bytes accessed | tf_op | source)
XLA Modules:
  0.0 93.8 jit_solution(6993623923136511111)
XLA Ops:
  0.6 89.2 %shard_map.94 = (bf16[2,3,16,768]{3,2,1,0:T(8,128)(2,1)S(1)}, bf16[768,3072]{1,0:T(8,128)(2,1)S(1)}, bf16[768,3072]{1,0:T(8,128)(2,1)S(1)}) custom-call(bf16[2,3,16,768]{3,2,1,0:T(8,128)(2,1)} %bitcast.7, bf16[2,3,16,768]{3,2,1,0:T(8,128)(2,1)} %bitcast.8, bf16[3,16,3072]{2,1,0:T(8,128)(2,1)} %bitcast.5, bf16[3,16,3072]{2,1,0:T(8,128)(2,1)} %bitcast.6, ...), custom_call_target="tpu_custom_call" | custom-call | flops 18119393280 | bytes 23592960 | tf_op jit(solution)/shard_map/pallas_call | solution.py:432
  89.8 3.8 %shard_map.95 = (bf16[2,3,16,768]{3,2,1,0:T(8,128)(2,1)}, bf16[768,3072]{1,0:T(8,128)(2,1)}, bf16[768,3072]{1,0:T(8,128)(2,1)}) custom-call(bf16[2,3,16,768]{3,2,1,0:T(8,128)(2,1)S(1)} %get-tuple-element.9.gi, bf16[768,3072]{1,0:T(8,128)(2,1)S(1)} %get-tuple-element.10.ga, bf16[768,3072]{1,0:T(8,128)(2,1)S(1)} %get-tuple-element.11.ua), custom_call_target="tpu_custom_call" | custom-call | tf_op jit(solution)/shard_map/pallas_call | solution.py:486

commit v4 on v3

--- a/solution.py
+++ b/solution.py
@@ -13,29 +13,35 @@
 NJ = 3
 TB = 16
 
-UNITS = ((0, 2048, 1024), (0, 0, 1024), (0, 1024, 1024), (1, 0, 1024), (1, 2048, 1024), (1, 1024, 1024), (2, 0, 1024), (2, 1024, 1024), (2, 2048, 1024))
-SUM_X_FIRST = (4, 3, 6, 2, 0)
-GATHER_X_FIRST = (1, 0, 7, 5)
-DIRECT_FIRST = False
+UNITS = ((0, 0, 768), (0, 2304, 768), (0, 1536, 768), (0, 768, 768), (1, 768, 768), (2, 0, 768), (1, 0, 768), (1, 1536, 768), (1, 2304, 768), (2, 2304, 768), (2, 1536, 768), (2, 768, 768))
+SUM_X_FIRST = (6, 0)
+GATHER_X_FIRST = (8, 11, 0, 4, 10)
+AHEAD = (0, 3, 2, 1)
 BLOCKS = tuple(sorted({(c0, w) for _, c0, w in UNITS}))
 WMAX = max(w for _, w in BLOCKS)
 
 ORDER = (
-    ("o0", 0), ("o1", 0), ("o0", 1), ("o1", 1), ("o0", 2), ("s0", 0), ("s0", 1), ("s0", 2),
-    ("s1", 0), ("s1", 1), ("o1", 2), ("i0", 0), ("s1", 2), ("s0", 3), ("s0", 4), ("s0", 5),
-    ("s1", 3), ("s1", 4), ("s1", 5), ("s2", 1), ("s2", 0), ("s0", 6), ("s0", 7), ("s0", 8),
-    ("s1", 6), ("s2", 2), ("s1", 7), ("i1", 0), ("s1", 8), ("s2", 3), ("s2", 5), ("s3", 0),
-    ("s3", 2), ("s2", 4), ("s3", 1), ("s2", 7), ("s2", 6), ("s2", 8), ("s3", 3), ("s3", 5),
-    ("s5", 0), ("s4", 0), ("s5", 2), ("s4", 2), ("s3", 4), ("s5", 1), ("s4", 1), ("s3", 6),
-    ("i2", 0), ("s3", 7), ("s4", 3), ("s3", 8), ("s5", 3), ("s4", 5), ("s5", 5), ("s7", 0),
-    ("s7", 2), ("s6", 0), ("s6", 2), ("s4", 4), ("s5", 4), ("s7", 1), ("s6", 1), ("s5", 6),
-    ("s4", 6), ("s5", 7), ("s4", 7), ("s6", 3), ("s4", 8), ("s5", 8), ("s7", 3), ("s7", 5),
-    ("s8", 2), ("s6", 5), ("s9", 2), ("s6", 4), ("s7", 4), ("s8", 0), ("s7", 6), ("s8", 1),
-    ("s9", 0), ("s6", 6), ("s9", 1), ("gs", 0), ("s6", 7), ("s7", 7), ("s8", 3), ("s6", 8),
-    ("s8", 5), ("s9", 3), ("s7", 8), ("s8", 4), ("s9", 5), ("s8", 6), ("s9", 4), ("gs", 1),
-    ("s8", 7), ("s8", 8), ("s9", 6), ("s9", 7), ("s9", 8), ("gs", 2), ("g10", 0), ("dw", 0),
-    ("dw", 1), ("dw", 2), ("g10", 1), ("dw", 3), ("g11", 0), ("dw", 4), ("g11", 2), ("dw", 5),
-    ("g11", 1),
+    ("o0", 0), ("p3", 0), ("p3", 1), ("p3", 2), ("p3", 3), ("p5", 0), ("o1", 0), ("o0", 1),
+    ("p5", 1), ("o1", 1), ("o0", 2), ("p5", 2), ("o1", 2), ("p5", 3), ("p7", 0), ("p7", 1),
+    ("s0", 0), ("p7", 2), ("s0", 1), ("p4", 0), ("p7", 3), ("s0", 2), ("s1", 0), ("p4", 1),
+    ("s1", 1), ("s0", 3), ("s1", 2), ("p4", 2), ("i1", 0), ("p4", 3), ("s0", 4), ("s1", 3),
+    ("s0", 6), ("s0", 7), ("s0", 8), ("p6", 0), ("s2", 1), ("s2", 0), ("s1", 4), ("p6", 1),
+    ("s0", 5), ("s0", 9), ("s2", 2), ("s1", 6), ("s1", 5), ("s0", 10), ("p8", 0), ("s0", 11),
+    ("s2", 3), ("s1", 7), ("p8", 1), ("s3", 0), ("s3", 1), ("p6", 2), ("p6", 3), ("s3", 2),
+    ("s2", 4), ("s1", 8), ("s2", 6), ("s2", 5), ("s1", 10), ("s1", 9), ("s5", 0), ("s3", 3),
+    ("s5", 1), ("p8", 2), ("s2", 7), ("p8", 3), ("s1", 11), ("s4", 0), ("s5", 2), ("s4", 1),
+    ("s4", 2), ("s3", 4), ("s7", 0), ("i2", 0), ("s5", 3), ("s7", 1), ("s2", 8), ("s3", 5),
+    ("s3", 6), ("s7", 2), ("s3", 7), ("s6", 1), ("s6", 2), ("s2", 10), ("s5", 4), ("s7", 3),
+    ("s2", 9), ("s3", 8), ("s6", 0), ("s5", 5), ("s4", 3), ("s5", 6), ("s5", 7), ("s8", 1),
+    ("s2", 11), ("s8", 2), ("s9", 1), ("s7", 4), ("s8", 0), ("s4", 4), ("s4", 5), ("s9", 2),
+    ("s5", 8), ("s7", 5), ("s6", 3), ("s7", 6), ("s4", 6), ("s4", 7), ("s9", 0), ("s7", 7),
+    ("s6", 4), ("s4", 8), ("s3", 10), ("s6", 5), ("s3", 9), ("s7", 8), ("s8", 3), ("s8", 4),
+    ("s3", 11), ("s6", 6), ("s9", 3), ("s6", 7), ("s5", 10), ("s6", 8), ("s4", 10), ("s9", 4),
+    ("s8", 5), ("s4", 9), ("gs", 0), ("s5", 9), ("s8", 8), ("s9", 5), ("s5", 11), ("s8", 6),
+    ("s4", 11), ("s9", 8), ("s7", 10), ("s8", 7), ("s9", 6), ("dw", 0), ("s7", 9), ("s7", 11),
+    ("s6", 9), ("s6", 10), ("s9", 7), ("gs", 1), ("s6", 11), ("dw", 1), ("s8", 10), ("g10", 0),
+    ("s8", 9), ("s8", 11), ("s9", 10), ("s9", 9), ("s9", 11), ("gs", 2), ("dw", 4), ("g11", 0),
+    ("dw", 5), ("g10", 1), ("dw", 6), ("dw", 7), ("dw", 2), ("dw", 3), ("g11", 1), ("g11", 2),
 )
 
 
@@ -65,6 +71,7 @@
     xg,
     xt,
     db,
+    hb,
     hs,
     hr,
     ho,
@@ -115,8 +122,6 @@
     peers = [dev_k, dev_zl, dev_zh]
     peers += [dev_x(d) for d in (1, 2, 3)]
     peers += [dev_y(d) for d in (1, 2, 3)]
-    if DIRECT_FIRST:
-        peers += [dev_y(d, True) for d in (1, 2, 3)]
     for dev in peers:
         pl.semaphore_signal(barrier, 1, device_id=dev, device_id_type=MESH)
 
@@ -132,6 +137,10 @@
     load("in", in_ref, xg.at[r])
     load("gp", gp_ref, gpv)
     load("up", up_ref, upv)
+    for u in AHEAD:
+        j, c0, w = UNITS[u]
+        for a, ref in ((0, gp_ref), (1, up_ref)):
+            load((u, a), ref.at[j, :, pl.ds(c0, w)], db.at[a, p, k, j, :, pl.ds(c0, w)])
     load("gw", gw_ref, gwv)
     load("uw", uw_ref, uwv)
     loaded = set()
@@ -158,23 +167,20 @@
         pltpu.make_async_copy(ref, ref, sem).wait()
 
     def o0(j):
-        src, dst = og_ref.at[:, j], og.at[r, :, j]
-        send(src, dst, 0, r_og.at[j, 0], dev_zh)
-        for d in (1, 3, 2):
-            send(src, dst, 0, r_og.at[j, 1], dev_y(d))
-        if j == 0 and DIRECT_FIRST:
-            for d in (1, 3, 2):
-                send(src, dst, 0, r_og.at[j, 1], dev_y(d, True))
+        if j == 0:
+            send(og_ref.at[:, j], og.at[r, :, j], 0, r_og.at[j, 0], dev_zh)
+        for d in (2, 1, 3):
+            send(og_ref.at[:, j], og.at[r, :, j], 0, r_og.at[j, 1], dev_y(d))
+        if j == 0:
+            for q in range(1, NJ):
+                send(og_ref.at[:, q], og.at[r, :, q], 0, r_og.at[q, 0], dev_zh)
+            send(in_ref, xg.at[r], 1, r_in.at[0], dev_zh)
 
     def o1(j):
         arrived(og.at[0, :, j], r_og.at[j, 0])
-        if j > 0 or not DIRECT_FIRST:
-            ref = og.at[rz, :, j]
-            for d in (1, 3, 2):
-                send(ref, ref, 0, r_og.at[j, 1], dev_y(d))
-
-    def i0(_):
-        send(in_ref, xg.at[r], 1, r_in.at[0], dev_zh)
+        ref = og.at[rz, :, j]
+        for d in (2, 1, 3):
+            send(ref, ref, 0, r_og.at[j, 1], dev_y(d))
 
     def i1(_):
         need("in")
@@ -258,17 +264,104 @@
                 xs[u, d - 1, 0] = (core_sum(u, zl * NX + q) + zr[u, q].astype(F32)).astype(BF16)
                 send(xs.at[u, d - 1, 0], xr.at[u, d - 1, 0], 3 + j, r_rs.at[u, 2], dev_x(d))
 
-    def piece(u, q):
-        return db.at[:, q, k, UNITS[u][0], :, cols_of(u)]
-
-    def pieces(u, n):
-        return db.at[:, pl.ds(0, n), 0, UNITS[u][0], :, cols_of(u)]
-
-    def part(u, a, q):
-        return db.at[a, q, k, UNITS[u][0], :, cols_of(u)]
-
-    def ag_send(u, n, ref, dev):
-        send(ref, ref, 3 + NJ + UNITS[u][0], r_ag.at[u, n], dev)
+    class Gather:
+        def __init__(self, u, kind):
+            self.u, self.sem = u, kind * len(UNITS) + u
+            if kind == 1:
+                self.sem = len(UNITS) + AHEAD.index(u)
+            self.send_sem = 3 + NJ + self.sem
+            self.hidden = kind == 0 and u in AHEAD
+
+        def piece(self, q):
+            if self.hidden:
+                return hb.at[AHEAD.index(self.u), q, k]
+            return db.at[:, q, k, UNITS[self.u][0], :, cols_of(self.u)]
+
+        def pieces(self, n):
+            if self.hidden:
+                return hb.at[AHEAD.index(self.u), pl.ds(0, n), 0]
+            return db.at[:, pl.ds(0, n), 0, UNITS[self.u][0], :, cols_of(self.u)]
+
+        def half(self, a, q):
+            if self.hidden:
+                h = WMAX // 2
+                return hb.at[AHEAD.index(self.u), q, k, :, pl.ds(a * h, h)]
+            return db.at[a, q, k, UNITS[self.u][0], :, cols_of(self.u)]
+
+        def send(self, n, ref, dev):
+            send(ref, ref, self.send_sem, r_ag.at[self.sem, n], dev)
+
+        def arrived(self, n, count):
+            arrived(self.pieces(count), r_ag.at[self.sem, n])
+
+        def sent(self):
+            if self.hidden:
+                ref = db.at[0, pl.ds(0, 5), 0, :, :, cols_of(self.u)]
+            else:
+                ref = db.at[:, pl.ds(0, 5), 0, :, :, cols_of(self.u)]
+            arrived(ref, send_sem.at[self.send_sem])
+
+    def g3(g):
+        ref = g.piece(p)
+        g.send(1, ref, dev_x(1))
+        g.send(1, ref, dev_x(3))
+        g.send(0, ref, dev_zl)
+        g.send(5, ref, dev_k)
+
+    def g4(g, x_first):
+        g.arrived(0, 1)
+        ref = g.piece(pz)
+        if not x_first:
+            g.send(2, ref, dev_x(1))
+            g.send(2, ref, dev_x(3))
+        g.send(5, ref, dev_k)
+
+    def sides(g, first, then, lane, relay, x_first):
+        lo = lane * NX + xmod(3)
+        hi = lane * NX + xmod(1)
+        g.arrived(first, 2)
+        if relay:
+            g.send(then, g.half(0, lo), dev_x(1))
+            g.send(then, g.half(1, hi), dev_x(3))
+        if relay and x_first:
+            g.send(2, g.piece(lo), dev_zl)
+            g.send(2, g.piece(hi), dev_zl)
+        g.send(5, g.piece(lo), dev_k)
+        g.send(5, g.piece(hi), dev_k)
+
+    def g5(g, x_first):
+        sides(g, 1, 3, zl, True, x_first)
+
+    def g6(g, x_first):
+        sides(g, 2, 4, 1 - zl, not x_first, x_first)
+
+    def g7(g, x_first):
+        g.arrived(3, 1)
+        ref = g.piece(zl * NX + xmod(2))
+        if x_first:
+            g.send(4, ref, dev_zl)
+        g.send(5, ref, dev_k)
+
+    def g8(g, x_first):
+        g.arrived(4, 1)
+        g.send(5, g.piece((1 - zl) * NX + xmod(2)), dev_k)
+
+    main = {u: Gather(u, 0) for u in range(len(UNITS))}
+    ahead = {u: Gather(u, 1) for u in AHEAD}
+
+    def p3(u):
+        need((u, 0), (u, 1))
+        g3(ahead[u])
+
+    def of_main(step):
+        return lambda u: step(main[u], u in GATHER_X_FIRST)
+
+    def of_ahead(step):
+        return lambda u: step(ahead[u], False)
+
+    def gradients(hidden, g, up):
+        s = jax.nn.sigmoid(g)
+        return hidden * up * s * (1.0 + g * (1.0 - s)), hidden * g * s
 
     def s3(u):
         need("gp", "up")
@@ -284,54 +377,15 @@
             lane = 0
         for d in (1, 2, 3):
             hidden = hidden + xr[u, d - 1, lane].astype(F32)
-        g = gpv[j, :, cols].astype(F32)
-        up = upv[j, :, cols].astype(F32)
-        s = jax.nn.sigmoid(g)
-        db[1, p, k, j, :, cols] = (hidden * g * s).astype(BF16)
-        db[0, p, k, j, :, cols] = (hidden * up * s * (1.0 + g * (1.0 - s))).astype(BF16)
-        ref = piece(u, p)
-        ag_send(u, 1, ref, dev_x(1))
-        ag_send(u, 1, ref, dev_x(3))
-        ag_send(u, 0, ref, dev_zl)
-        ag_send(u, 5, ref, dev_k)
-
-    def s4(u):
-        arrived(pieces(u, 1), r_ag.at[u, 0])
-        ref = piece(u, pz)
-        if u not in GATHER_X_FIRST:
-            ag_send(u, 2, ref, dev_x(1))
-            ag_send(u, 2, ref, dev_x(3))
-        ag_send(u, 5, ref, dev_k)
-
-    def sides(u, first, then, lane, relay):
-        lo = lane * NX + xmod(3)
-        hi = lane * NX + xmod(1)
-        arrived(pieces(u, 2), r_ag.at[u, first])
-        if relay:
-            ag_send(u, then, part(u, 0, lo), dev_x(1))
-            ag_send(u, then, part(u, 1, hi), dev_x(3))
-        if relay and u in GATHER_X_FIRST:
-            ag_send(u, 2, piece(u, lo), dev_zl)
-            ag_send(u, 2, piece(u, hi), dev_zl)
-        ag_send(u, 5, piece(u, lo), dev_k)
-        ag_send(u, 5, piece(u, hi), dev_k)
-
-    def s5(u):
-        sides(u, 1, 3, zl, True)
-
-    def s6(u):
-        sides(u, 2, 4, 1 - zl, u not in GATHER_X_FIRST)
-
-    def s7(u):
-        arrived(pieces(u, 1), r_ag.at[u, 3])
-        ref = piece(u, zl * NX + xmod(2))
-        if u in GATHER_X_FIRST:
-            ag_send(u, 4, ref, dev_zl)
-        ag_send(u, 5, ref, dev_k)
-
-    def s8(u):
-        arrived(pieces(u, 1), r_ag.at[u, 4])
-        ag_send(u, 5, piece(u, (1 - zl) * NX + xmod(2)), dev_k)
+        if u in AHEAD:
+            hb[AHEAD.index(u), p, k] = hidden.astype(BF16)
+        else:
+            g = gpv[j, :, cols].astype(F32)
+            up = upv[j, :, cols].astype(F32)
+            dgate, dup = gradients(hidden, g, up)
+            db[0, p, k, j, :, cols] = dgate.astype(BF16)
+            db[1, p, k, j, :, cols] = dup.astype(BF16)
+        g3(main[u])
 
     begun = set()
 
@@ -339,7 +393,21 @@
         j, c0, w = UNITS[u]
         cols = cols_of(u)
         need("gw", "uw")
-        arrived(pieces(u, NP), r_ag.at[u, 5])
+        main[u].arrived(5, NP)
+        if u in AHEAD:
+            ahead[u].arrived(5, NP)
+            ahead[u].sent()
+
+            def make(n, _):
+                q, kk = n // NK, n % NK
+                g = db[0, q, kk, j, :, cols].astype(F32)
+                up = db[1, q, kk, j, :, cols].astype(F32)
+                dgate, dup = gradients(hb[AHEAD.index(u), q, kk].astype(F32), g, up)
+                db[0, q, kk, j, :, cols] = dgate.astype(BF16)
+                db[1, q, kk, j, :, cols] = dup.astype(BF16)
+                return 0
+
+            lax.fori_loop(0, NP * NK, make, 0)
         dgate = db[0, :, :, j, :, cols].reshape(NP * NK * TB, w)
         dup = db[1, :, :, j, :, cols].reshape(NP * NK * TB, w)
         out = right_trans(dgate, gwv[:, cols]) + right_trans(dup, uwv[:, cols])
@@ -394,16 +462,20 @@
         (ga_ref, ua_ref)[n % 2][:, cols] = out.astype(BF16)
 
     steps = dict(
-        o0=o0, o1=o1, i0=i0, i1=i1, i2=i2, s0=s0, s1=s1, s2=s2, s3=s3, s4=s4, s5=s5, s6=s6,
-        s7=s7, s8=s8, s9=s9, gs=gs0, g10=g10, g11=g11, dw=dw,
+        o0=o0, o1=o1, i1=i1, i2=i2, s0=s0, s1=s1, s2=s2, s3=s3, s9=s9, gs=gs0, g10=g10, g11=g11,
+        dw=dw, p3=p3,
     )
+    for n, step in enumerate((g4, g5, g6, g7, g8)):
+        steps["s" + str(4 + n)] = of_main(step)
+        steps["p" + str(4 + n)] = of_ahead(step)
     for name, arg in ORDER:
         steps[name](arg)
     for n in range(3):
         arrived(og.at[pl.ds(0, 7)], send_sem.at[n])
     for j in range(NJ):
         arrived(db.at[0, pl.ds(0, 5), 0], send_sem.at[3 + j])
-        arrived(db.at[:, pl.ds(0, 5), 0], send_sem.at[3 + NJ + j])
+    for g in main.values():
+        g.sent()
 
 
 def store(gi, ga, ua, gi_out, ga_out, ua_out, sem):
@@ -448,6 +520,7 @@
             vm((NP, NK, NJ, TB, dl), BF16),
             vm((dl, tok), BF16),
             vm((2, NP, NK, NJ, TB, ff), BF16),
+            vm((max(1, len(AHEAD)), NP, NK, TB, WMAX), BF16),
             vm((nu, NP, TB, WMAX), BF16),
             vm((nu, NP, TB, WMAX), BF16),
             vm((nu, NP, TB, WMAX), F32),
@@ -460,12 +533,12 @@
             vm((NJ, 3, 2, NK, TB, dl), BF16),
             vm((NJ, NK, TB, dl), BF16),
             vm((NJ, NK, TB, dl), BF16),
-            dma((7,)),
-            dma((3 + 2 * NJ,)),
+            dma((7 + 2 * len(AHEAD),)),
+            dma((3 + NJ + nu + len(AHEAD),)),
             dma((NJ, 2)),
             dma((2,)),
             dma((nu, 3)),
-            dma((nu, 6)),
+            dma((nu + len(AHEAD), 6)),
             dma((NJ, 2)),
         ],
         compiler_params=pltpu.CompilerParams(

time: 93.9 us -> 89.3 us (0.951)
  Pallas kernels: 92.9 us -> 88.4 us
    pallas_call x1, Pallas kernels: 89.2 us -> 84.7 us  [on_device(): pl.pallas_call(kernel, out_shape=(pltpu.VMEM((NK, NJ, TB, dl), BF16), plt...]
where the time goes in v4:
time: 89.3 us; the launch traced here: 89.2 us
  Pallas kernels  88.4 us (99%)
    pallas_call x1, Pallas kernels, on_device(): pl.pallas_call(kernel, out_shape=(pltpu.VMEM((NK, NJ, TB, dl), BF16), plt...  84.7 us
    pallas_call x1, Pallas kernels, on_device(): pl.pallas_call(store, out_shape=(jax.ShapeDtypeStruct((NK, NJ, TB, dl), B...  3.76 us

profile of v4, /device:TPU:1, one launch (start us, length us, event | category | flops | bytes accessed | tf_op | source)
XLA Modules:
  0.0 89.2 jit_solution(1820419966864604292)
XLA Ops:
  0.6 84.7 %shard_map.94 = (bf16[2,3,16,768]{3,2,1,0:T(8,128)(2,1)S(1)}, bf16[768,3072]{1,0:T(8,128)(2,1)S(1)}, bf16[768,3072]{1,0:T(8,128)(2,1)S(1)}) custom-call(bf16[2,3,16,768]{3,2,1,0:T(8,128)(2,1)} %bitcast.7, bf16[2,3,16,768]{3,2,1,0:T(8,128)(2,1)} %bitcast.8, bf16[3,16,3072]{2,1,0:T(8,128)(2,1)} %bitcast.5, bf16[3,16,3072]{2,1,0:T(8,128)(2,1)} %bitcast.6, ...), custom_call_target="tpu_custom_call" | custom-call | flops 18119393280 | bytes 23592960 | tf_op jit(solution)/shard_map/pallas_call | solution.py:504
  85.3 3.8 %shard_map.95 = (bf16[2,3,16,768]{3,2,1,0:T(8,128)(2,1)}, bf16[768,3072]{1,0:T(8,128)(2,1)}, bf16[768,3072]{1,0:T(8,128)(2,1)}) custom-call(bf16[2,3,16,768]{3,2,1,0:T(8,128)(2,1)S(1)} %get-tuple-element.9.gi, bf16[768,3072]{1,0:T(8,128)(2,1)S(1)} %get-tuple-element.10.ga, bf16[768,3072]{1,0:T(8,128)(2,1)S(1)} %get-tuple-element.11.ua), custom_call_target="tpu_custom_call" | custom-call | tf_op jit(solution)/shard_map/pallas_call | solution.py:559

commit v5 on v4

--- a/solution.py
+++ b/solution.py
@@ -21,27 +21,27 @@
 WMAX = max(w for _, w in BLOCKS)
 
 ORDER = (
-    ("o0", 0), ("p3", 0), ("p3", 1), ("p3", 2), ("p3", 3), ("p5", 0), ("o1", 0), ("o0", 1),
-    ("p5", 1), ("o1", 1), ("o0", 2), ("p5", 2), ("o1", 2), ("p5", 3), ("p7", 0), ("p7", 1),
-    ("s0", 0), ("p7", 2), ("s0", 1), ("p4", 0), ("p7", 3), ("s0", 2), ("s1", 0), ("p4", 1),
-    ("s1", 1), ("s0", 3), ("s1", 2), ("p4", 2), ("i1", 0), ("p4", 3), ("s0", 4), ("s1", 3),
-    ("s0", 6), ("s0", 7), ("s0", 8), ("p6", 0), ("s2", 1), ("s2", 0), ("s1", 4), ("p6", 1),
-    ("s0", 5), ("s0", 9), ("s2", 2), ("s1", 6), ("s1", 5), ("s0", 10), ("p8", 0), ("s0", 11),
-    ("s2", 3), ("s1", 7), ("p8", 1), ("s3", 0), ("s3", 1), ("p6", 2), ("p6", 3), ("s3", 2),
-    ("s2", 4), ("s1", 8), ("s2", 6), ("s2", 5), ("s1", 10), ("s1", 9), ("s5", 0), ("s3", 3),
-    ("s5", 1), ("p8", 2), ("s2", 7), ("p8", 3), ("s1", 11), ("s4", 0), ("s5", 2), ("s4", 1),
-    ("s4", 2), ("s3", 4), ("s7", 0), ("i2", 0), ("s5", 3), ("s7", 1), ("s2", 8), ("s3", 5),
-    ("s3", 6), ("s7", 2), ("s3", 7), ("s6", 1), ("s6", 2), ("s2", 10), ("s5", 4), ("s7", 3),
-    ("s2", 9), ("s3", 8), ("s6", 0), ("s5", 5), ("s4", 3), ("s5", 6), ("s5", 7), ("s8", 1),
-    ("s2", 11), ("s8", 2), ("s9", 1), ("s7", 4), ("s8", 0), ("s4", 4), ("s4", 5), ("s9", 2),
-    ("s5", 8), ("s7", 5), ("s6", 3), ("s7", 6), ("s4", 6), ("s4", 7), ("s9", 0), ("s7", 7),
-    ("s6", 4), ("s4", 8), ("s3", 10), ("s6", 5), ("s3", 9), ("s7", 8), ("s8", 3), ("s8", 4),
-    ("s3", 11), ("s6", 6), ("s9", 3), ("s6", 7), ("s5", 10), ("s6", 8), ("s4", 10), ("s9", 4),
-    ("s8", 5), ("s4", 9), ("gs", 0), ("s5", 9), ("s8", 8), ("s9", 5), ("s5", 11), ("s8", 6),
-    ("s4", 11), ("s9", 8), ("s7", 10), ("s8", 7), ("s9", 6), ("dw", 0), ("s7", 9), ("s7", 11),
-    ("s6", 9), ("s6", 10), ("s9", 7), ("gs", 1), ("s6", 11), ("dw", 1), ("s8", 10), ("g10", 0),
-    ("s8", 9), ("s8", 11), ("s9", 10), ("s9", 9), ("s9", 11), ("gs", 2), ("dw", 4), ("g11", 0),
-    ("dw", 5), ("g10", 1), ("dw", 6), ("dw", 7), ("dw", 2), ("dw", 3), ("g11", 1), ("g11", 2),
+    ("o0", 0), ("p3", 0), ("p3", 3), ("p3", 1), ("p3", 2), ("o1", 0), ("p5", 0), ("o0", 1),
+    ("p5", 2), ("o1", 1), ("p5", 1), ("o0", 2), ("p5", 3), ("s0", 0), ("s0", 1), ("p4", 0),
+    ("s0", 2), ("s1", 0), ("s1", 1), ("s0", 3), ("p4", 1), ("o1", 2), ("p4", 2), ("s1", 2),
+    ("p7", 1), ("s0", 4), ("s1", 3), ("s0", 7), ("i1", 0), ("p6", 0), ("p4", 3), ("s0", 6),
+    ("s2", 1), ("s1", 6), ("s1", 4), ("s2", 0), ("s0", 5), ("s0", 8), ("s2", 2), ("s1", 5),
+    ("p6", 3), ("s2", 3), ("s0", 10), ("p7", 2), ("s3", 1), ("p6", 2), ("s1", 7), ("s0", 11),
+    ("s3", 0), ("s2", 4), ("s2", 6), ("s3", 2), ("s2", 5), ("s0", 9), ("s1", 8), ("p6", 1),
+    ("s3", 3), ("s1", 10), ("s4", 1), ("s2", 7), ("s5", 1), ("s3", 6), ("s5", 0), ("s4", 2),
+    ("s1", 11), ("s1", 9), ("s3", 4), ("s6", 1), ("s4", 3), ("s2", 8), ("s5", 2), ("s3", 5),
+    ("s7", 0), ("s5", 3), ("s7", 1), ("s3", 7), ("s5", 4), ("s6", 2), ("p8", 1), ("s8", 1),
+    ("s2", 10), ("s9", 1), ("s3", 8), ("s7", 3), ("s6", 3), ("s7", 2), ("p7", 0), ("p7", 3),
+    ("s4", 0), ("p8", 2), ("s5", 6), ("s2", 11), ("i2", 0), ("p8", 0), ("p8", 3), ("s6", 0),
+    ("s2", 9), ("s4", 6), ("s4", 5), ("s7", 4), ("s8", 0), ("s5", 8), ("s8", 3), ("s5", 5),
+    ("s8", 2), ("s9", 0), ("s4", 7), ("s3", 10), ("s9", 2), ("s6", 4), ("s6", 5), ("s6", 6),
+    ("s3", 9), ("s4", 4), ("s7", 8), ("s8", 4), ("s3", 11), ("s9", 3), ("s7", 6), ("s6", 7),
+    ("s7", 5), ("s9", 4), ("s8", 5), ("s5", 7), ("s8", 6), ("s5", 10), ("gs", 0), ("s4", 9),
+    ("s4", 8), ("s9", 5), ("s6", 8), ("s8", 8), ("s5", 11), ("s5", 9), ("s9", 6), ("s8", 7),
+    ("s9", 8), ("s7", 10), ("s7", 7), ("dw", 0), ("s7", 11), ("s6", 9), ("s4", 10), ("s9", 7),
+    ("gs", 1), ("s6", 10), ("dw", 1), ("s8", 10), ("g10", 0), ("s4", 11), ("s7", 9), ("s6", 11),
+    ("s8", 9), ("s8", 11), ("s9", 10), ("s9", 9), ("s9", 11), ("gs", 2), ("dw", 5), ("dw", 4),
+    ("g11", 0), ("g10", 1), ("dw", 2), ("dw", 7), ("dw", 3), ("dw", 6), ("g11", 1), ("g11", 2),
 )
 
 
@@ -235,7 +235,7 @@
         j = UNITS[u][0]
         arrived(hr.at[u], r_rs.at[u, 0])
         if u in SUM_X_FIRST:
-            for d in (1, 3, 2):
+            for d in (2, 1, 3):
                 for lane in range(NZL):
                     xs[u, d - 1, lane] = core_sum(u, lane * NX + xmod(d)).astype(BF16)
                 send(xs.at[u, d - 1], xr.at[u, d - 1], 3 + j, r_rs.at[u, 1], dev_x(d))
@@ -259,7 +259,7 @@
             send(zs.at[u, 0], zr.at[u, 0], 3 + j, r_rs.at[u, 2], dev_zl)
         else:
             arrived(zr.at[u], r_rs.at[u, 1])
-            for d in (1, 3, 2):
+            for d in (2, 1, 3):
                 q = xmod(d)
                 xs[u, d - 1, 0] = (core_sum(u, zl * NX + q) + zr[u, q].astype(F32)).astype(BF16)
                 send(xs.at[u, d - 1, 0], xr.at[u, d - 1, 0], 3 + j, r_rs.at[u, 2], dev_x(d))
@@ -418,15 +418,18 @@
 
     def gs0(j):
         gs[j] = gacc[j].astype(BF16).reshape(NP, NK, TB, dl)
-        for d in (1, 3, 2):
-            q = ymod(d) * 2
-            if j < NJ - 1:
-                send(gs.at[j, pl.ds(q, 2)], gr.at[j, d - 1], 2, r_gi.at[j, 1], dev_y(d))
-            else:
-                send(gs.at[j, q + zh], gr.at[j, d - 1, 0], 2, r_gi.at[j, 1], dev_y(d))
-                send(gs.at[j, q + 1 - zh], gr.at[j, d - 1, 1], 2, r_gi.at[j, 1], dev_y(d, True))
         if j == NJ - 1:
-            send(gs.at[j, rz], gzr.at[j], 2, r_gi.at[j, 0], dev_zh)
+            for other in (True, False):
+                for d in (2, 1, 3):
+                    q = ymod(d) * 2 + (1 - zh if other else zh)
+                    slot = gr.at[j, d - 1, int(other)]
+                    send(gs.at[j, q], slot, 2, r_gi.at[j, 1], dev_y(d, other))
+                if other:
+                    send(gs.at[j, rz], gzr.at[j], 2, r_gi.at[j, 0], dev_zh)
+        else:
+            for d in (2, 1, 3):
+                rows = gs.at[j, pl.ds(ymod(d) * 2, 2)]
+                send(rows, gr.at[j, d - 1], 2, r_gi.at[j, 1], dev_y(d))
 
     def rows_of(dest):
         return pl.ds(pl.multiple_of(dest * NK * TB, NK * TB), NK * TB)

time: 89.3 us -> 89 us (level)
  no operation moved by 1% of the time
where the time goes in v5:
time: 89 us; the launch traced here: 88.9 us
  Pallas kernels  88.1 us (99%)
    pallas_call x1, Pallas kernels, on_device(): pl.pallas_call(kernel, out_shape=(pltpu.VMEM((NK, NJ, TB, dl), BF16), plt...  84.3 us
    pallas_call x1, Pallas kernels, on_device(): pl.pallas_call(store, out_shape=(jax.ShapeDtypeStruct((NK, NJ, TB, dl), B...  3.76 us

profile of v5, /device:TPU:1, one launch (start us, length us, event | category | flops | bytes accessed | tf_op | source)
XLA Modules:
  0.0 88.9 jit_solution(18440080583665126522)
XLA Ops:
  0.6 84.3 %shard_map.94 = (bf16[2,3,16,768]{3,2,1,0:T(8,128)(2,1)S(1)}, bf16[768,3072]{1,0:T(8,128)(2,1)S(1)}, bf16[768,3072]{1,0:T(8,128)(2,1)S(1)}) custom-call(bf16[2,3,16,768]{3,2,1,0:T(8,128)(2,1)} %bitcast.7, bf16[2,3,16,768]{3,2,1,0:T(8,128)(2,1)} %bitcast.8, bf16[3,16,3072]{2,1,0:T(8,128)(2,1)} %bitcast.5, bf16[3,16,3072]{2,1,0:T(8,128)(2,1)} %bitcast.6, ...), custom_call_target="tpu_custom_call" | custom-call | flops 18119393280 | bytes 23592960 | tf_op jit(solution)/shard_map/pallas_call | solution.py:507
  84.9 3.8 %shard_map.95 = (bf16[2,3,16,768]{3,2,1,0:T(8,128)(2,1)}, bf16[768,3072]{1,0:T(8,128)(2,1)}, bf16[768,3072]{1,0:T(8,128)(2,1)}) custom-call(bf16[2,3,16,768]{3,2,1,0:T(8,128)(2,1)S(1)} %get-tuple-element.9.gi, bf16[768,3072]{1,0:T(8,128)(2,1)S(1)} %get-tuple-element.10.ga, bf16[768,3072]{1,0:T(8,128)(2,1)S(1)} %get-tuple-element.11.ua), custom_call_target="tpu_custom_call" | custom-call | tf_op jit(solution)/shard_map/pallas_call | solution.py:562
